TPU v7x, 32 devices: a whole 2x2x4 slice. The times are simulated.
32 devices in a mesh: groups: 2 (over x), gz: 16 (over z, y, core).
Axes of the slice: x: 2, y: 2, z: 4, core: 2. Of those that a mesh axis runs over, the one named last changes fastest.
Arguments:
- waves: bfloat16 [192, 8, 64, 256], P(('groups', 'gz')), parts along dimension 0, may hold values from -6 to 6
- potential: float32 [192, 512], P(('groups', 'gz')), parts along dimension 0, may hold values from 0.25 to 4
- domain_of: int32 [32], P('groups'), parts along dimension 0, may hold values from 0 to 7, never falling along the last dimension, each value on 1 to 9 neighbouring positions
Outputs:
- orbitals: bfloat16 [192, 8, 64, 256], P(('groups', 'gz')), parts along dimension 0
There are 2 independent parts, one for each index of `groups`. A program takes and returns all parts, laid end to end along the dimension named above; each array names one. Nothing has to cross between parts.
Inputs may be any that keep to these rules, and one draw needn't show every extreme that they name: `domain_of`: never falls; every domain holds 1 to 9 blocks, one domain exactly that many.
All inputs are finite; a program needn't handle non-finite values.
Results may differ from a plain program's by a relative error of at most 0.0038.
The roundings to bfloat16 on the way count: a program that leaves them out, or rounds other values in their place, can miss the bound.
Values may be sent and summed in bfloat16 or wider, within the bound.
A program may use at most 64 MiB of HBM per device.

v0:
```python
import jax
import jax.numpy as jnp
from jax import lax
from jax.sharding import PartitionSpec as P

PANEL = 128
NX = 64
NY = 8
DOMS = 8
DEGREE = 4


COEF = (-49.0 / 18.0, 1.5, -0.15, 1.0 / 90.0)
CSHIFT = 7.0
EWIDTH = 5.0


def extended_2(block, sides, width):
    for axis, dim in sides:
        count = lax.axis_size(axis)
        forward = [(i, i + 1) for i in range(count - 1)]
        backward = [(target, source) for source, target in forward]
        low = lax.ppermute(
            lax.slice_in_dim(block, block.shape[dim] - width, None, axis=dim), axis, forward
        )
        high = lax.ppermute(lax.slice_in_dim(block, 0, width, axis=dim), axis, backward)
        block = jnp.concatenate([low, block, high], axis=dim)
    return block


def hamiltonian(extended, potential):
    inner = extended[3:-3]
    planes = inner.shape[0]
    rows_y = inner.shape[1]
    rows_x = inner.shape[2]
    padded_y = jnp.pad(inner, ((0, 0), (3, 3), (0, 0), (0, 0)))
    padded_x = jnp.pad(inner, ((0, 0), (0, 0), (3, 3), (0, 0)))
    total = 3.0 * COEF[0] * inner
    for distance in (1, 2, 3):
        along_z = (
            extended[3 + distance : 3 + distance + planes]
            + extended[3 - distance : 3 - distance + planes]
        )
        along_y = (
            padded_y[:, 3 + distance : 3 + distance + rows_y]
            + padded_y[:, 3 - distance : 3 - distance + rows_y]
        )
        along_x = (
            padded_x[:, :, 3 + distance : 3 + distance + rows_x]
            + padded_x[:, :, 3 - distance : 3 - distance + rows_x]
        )
        total = total + COEF[distance] * (along_z + along_y + along_x)
    return potential[:, :, :, None] * inner - 0.5 * total


def shards(waves, potential, domain_of):
    slabs = lax.axis_size("gz")
    position = lax.axis_index("gz")
    planes = waves.shape[0]
    bands = waves.shape[3]
    grid = potential.reshape(planes, NY, NX)
    owner = domain_of[position]
    below = jnp.where(position > 0, domain_of[jnp.maximum(position - 1, 0)] == owner, False).astype(
        jnp.float32
    )
    above = jnp.where(
        position < slabs - 1, domain_of[jnp.minimum(position + 1, slabs - 1)] == owner, False
    ).astype(jnp.float32)
    mask_three = jnp.concatenate(
        [
            jnp.broadcast_to(below, (3,)),
            jnp.ones((planes,), jnp.float32),
            jnp.broadcast_to(above, (3,)),
        ]
    )[:, None, None, None]

    def rimmed(field):
        return extended_2(field, (("gz", 0),), 3).astype(jnp.float32) * mask_three

    extended = rimmed(waves)
    image = hamiltonian(extended, grid)
    older = waves
    current = ((image - CSHIFT * extended[3:-3]) / EWIDTH).astype(jnp.bfloat16)
    for turn in range(DEGREE - 1):
        extended = rimmed(current)
        image = hamiltonian(extended, grid)
        newer = (
            2.0 / EWIDTH * (image - CSHIFT * extended[3:-3]) - older.astype(jnp.float32)
        ).astype(jnp.bfloat16)
        older, current = (current, newer)
    cells = jnp.sum((domain_of == owner).astype(jnp.float32)) * (planes * NY * NX)
    rows = current.reshape(planes * NY * NX, bands)

    def domain_total(term):
        picker = (jnp.arange(DOMS) == owner).astype(jnp.float32)
        summed = lax.psum(picker[:, None, None] * term[None], "gz")
        return jnp.sum(picker[:, None, None] * summed, axis=0)

    identity = jnp.eye(PANEL, dtype=jnp.float32)
    pieces = []
    for panel in range(bands // PANEL):
        block = rows[:, panel * PANEL : (panel + 1) * PANEL]
        if panel > 0:
            earlier = pieces[0]
            correlation = (
                domain_total(
                    jnp.einsum("ca,cb->ab", earlier, block, preferred_element_type=jnp.float32)
                )
                / cells
            )
            block = (
                block.astype(jnp.float32)
                - jnp.dot(
                    earlier, correlation.astype(jnp.bfloat16), preferred_element_type=jnp.float32
                )
            ).astype(jnp.bfloat16)
        gram = (
            domain_total(jnp.einsum("ca,cb->ab", block, block, preferred_element_type=jnp.float32))
            / cells
        )
        factor = jnp.linalg.cholesky(gram)
        inverse = jax.scipy.linalg.solve_triangular(factor, identity, lower=True)
        whitening = inverse.T.astype(jnp.bfloat16)
        pieces.append(
            jnp.dot(block, whitening, preferred_element_type=jnp.float32).astype(jnp.bfloat16)
        )
    return jnp.concatenate(pieces, axis=1).reshape(planes, NY, NX, bands)


def solution(mesh):
    return jax.shard_map(
        shards,
        mesh=mesh,
        in_specs=(P(("groups", "gz"), None, None, None), P(("groups", "gz"), None), P("groups")),
        out_specs=P(("groups", "gz"), None, None, None),
        check_vma=False,
    )
```

profile of v0, /device:TPU:0, one launch (start us, length us, event | category | flops | bytes accessed | tf_op | source)
XLA Modules:
  0.0 490.9 jit_solution(13511593628192767567)
XLA Ops:
  6.5 2.8 fusion.114
  9.3 2.4 collective-permute-start
  11.7 1.3 collective-permute-start.1
  13.1 0.7 fusion.115
  16.2 2.0 collective-permute-done.1
  18.2 0.7 convert_multiply_fusion.3
  19.0 0.2 slice.356
  19.2 6.6 %fusion.11 = bf16[6,8,64,256]{3,2,1,0:T(8,128)(2,1)S(1)} fusion(f32[6,8,64,256]{3,2,1,0:T(8,128)S(1)} %slice.356, f32[12,8,64,256]{3,2,1,0:T(8,128)S(1)} %convert_multiply_fusion.3, f32[6,8,64]{2,1,0:T(8,128)S(1)} %mul.191), kind=kLoop, calls=%fused_computation.66 | loop fusion | flops 22806528 | bytes 23605248 | tf_op jit(solution)/shard_map/convert_element_type | solution.py:83
  25.8 0.2 fusion.113
  25.9 15.7 %collective-permute-start.2 = (bf16[3,8,64,256]{3,2,1,0:T(8,128)(2,1)S(1)}, bf16[3,8,64,256]{3,2,1,0:T(8,128)(2,1)S(1)}, u32[]{:S(2)}, u32[]{:S(2)}) collective-permute-start(bf16[3,8,64,256]{3,2,1,0:T(8,128)(2,1)S(1)} %get-tuple-element.11), channel_id=1, source_target_pairs={{0,1},{1,2},{2,3},{3,4},{4,5},{5,6},{6,7},{7,8},{8,9},{9,10},{10,1... | collective-permute-start | bytes 2359304 | tf_op jit(solution)/shard_map/ppermute | solution.py:23
  41.7 1.3 collective-permute-start.3
  43.0 0.5 collective-permute-done.2
  43.5 4.2 collective-permute-done.3
  47.7 0.7 convert_multiply_fusion.2
  48.4 2.0 slice.365
  50.4 18.8 %fusion.95 = bf16[6,8,64,256]{3,2,1,0:T(8,128)(2,1)S(1)} fusion(bf16[6,8,64,256]{3,2,1,0:T(8,128)(2,1)S(1)} %copy-done, f32[6,8,64,256]{3,2,1,0:T(8,128)} %slice.365, f32[12,8,64,256]{3,2,1,0:T(8,128)S(1)} %convert_multiply_fusion.2, f32[6,8,64]{2,1,0:T(8,128)S(1)} %mul.191), kind=kLoop, calls=%fused_computation.162 | loop fusion | flops 24379392 | bytes 25178112 | tf_op jit(solution)/shard_map/convert_element_type | solution.py:89
  69.3 0.2 fusion.112
  69.5 15.6 %collective-permute-start.4 = (bf16[3,8,64,256]{3,2,1,0:T(8,128)(2,1)S(1)}, bf16[3,8,64,256]{3,2,1,0:T(8,128)(2,1)S(1)}, u32[]{:S(2)}, u32[]{:S(2)}) collective-permute-start(bf16[3,8,64,256]{3,2,1,0:T(8,128)(2,1)S(1)} %get-tuple-element.9), channel_id=1, source_target_pairs={{0,1},{1,2},{2,3},{3,4},{4,5},{5,6},{6,7},{7,8},{8,9},{9,10},{10,1... | collective-permute-start | bytes 2359304 | tf_op jit(solution)/shard_map/ppermute | solution.py:23
  85.1 1.3 collective-permute-start.5
  86.4 0.5 collective-permute-done.4
  86.9 4.3 collective-permute-done.5
  91.2 0.7 convert_multiply_fusion.1
  92.0 2.0 slice.374
  94.0 18.8 %fusion.94 = bf16[6,8,64,256]{3,2,1,0:T(8,128)(2,1)S(1)} fusion(bf16[6,8,64,256]{3,2,1,0:T(8,128)(2,1)S(1)} %fusion.11, f32[6,8,64,256]{3,2,1,0:T(8,128)} %slice.374, f32[12,8,64,256]{3,2,1,0:T(8,128)S(1)} %convert_multiply_fusion.1, f32[6,8,64]{2,1,0:T(8,128)S(1)} %mul.191), kind=kLoop, calls=%fused_computation.161 | loop fusion | flops 24379392 | bytes 25178112 | tf_op jit(solution)/shard_map/convert_element_type | solution.py:89
  112.8 0.2 fusion.111
  113.0 15.6 %collective-permute-start.6 = (bf16[3,8,64,256]{3,2,1,0:T(8,128)(2,1)S(1)}, bf16[3,8,64,256]{3,2,1,0:T(8,128)(2,1)S(1)}, u32[]{:S(2)}, u32[]{:S(2)}) collective-permute-start(bf16[3,8,64,256]{3,2,1,0:T(8,128)(2,1)S(1)} %get-tuple-element.6), channel_id=1, source_target_pairs={{0,1},{1,2},{2,3},{3,4},{4,5},{5,6},{6,7},{7,8},{8,9},{9,10},{10,1... | collective-permute-start | bytes 2359304 | tf_op jit(solution)/shard_map/ppermute | solution.py:23
  128.6 1.3 collective-permute-start.7
  129.9 0.5 compare_convert_fusion.1
  130.5 4.3 collective-permute-done.7
  134.7 0.7 convert_multiply_fusion
  135.5 0.3 slice.383
  135.8 6.8 %fusion.93 = bf16[6,8,64,256]{3,2,1,0:T(8,128)(2,1)S(1)} fusion(bf16[6,8,64,256]{3,2,1,0:T(8,128)(2,1)S(1)} %fusion.95, f32[6,8,64,256]{3,2,1,0:T(8,128)S(1)} %slice.383, f32[12,8,64,256]{3,2,1,0:T(8,128)S(1)} %convert_multiply_fusion, f32[6,8,64]{2,1,0:T(8,128)S(1)} %mul.191), kind=kLoop, calls=%fused_computation.160 | loop fusion | flops 24379392 | bytes 25178112 | tf_op jit(solution)/shard_map/convert_element_type | solution.py:89
  142.6 0.4 fusion.99
  143.0 0.9 broadcast_multiply_fusion.2
  143.9 0.2 all-reduce.14.cloned.1.call-start
  144.2 1.2 fusion.110
  146.1 100.8 %all-reduce.12.cloned.1.call-done = f32[8,128,128]{2,1,0:T(8,128)} async-done(((f32[8,128,128]{2,1,0:T(8,128)}), f32[8,128,128]{2,1,0:T(8,128)}) %all-reduce.12.cloned.1.call-update) | async-done | bytes 524304 | tf_op jit(solution)/shard_map/psum | solution.py:96
  246.8 1.1 multiply_reduce_fusion.2
  248.0 0.1 copy.10
  248.1 0.1 copy.11
  248.2 11.7 %cholesky.44 = f32[128,128]{1,0:T(8,128)S(1)} custom-call(f32[128,128]{1,0:T(8,128)S(1)} %fusion.108), custom_call_target="Cholesky" | custom-call | tf_op jit(solution)/shard_map/jit(cholesky)/cholesky | solution.py:121
  260.0 0.6 compare_reduce_fusion.1
  260.6 0.7 fusion.103
  261.3 9.8 %custom-call.6 = f32[1,128,128]{1,2,0:T(8,128)S(1)} custom-call(f32[1,128,128]{2,1,0:T(8,128)S(1)} %fusion.103), custom_call_target="InvertDiagBlocksLowerTriangular" | custom-call | tf_op jit(solution)/shard_map/jit(_solve_triangular)/triangular_solve | solution.py:122
  271.1 0.3 convolution_convert_fusion.3
  271.4 0.4 convolution_convert_fusion.1
  271.8 0.4 fusion.96
  272.1 0.9 broadcast_multiply_fusion.1
  273.1 0.3 all-reduce.16.cloned.1.call-start
  273.3 90.4 %all-reduce.14.cloned.1.call-done = f32[8,128,128]{2,1,0:T(8,128)} async-done(((f32[8,128,128]{2,1,0:T(8,128)}), f32[8,128,128]{2,1,0:T(8,128)}) %all-reduce.14.cloned.1.call-update) | async-done | bytes 524304 | tf_op jit(solution)/shard_map/psum | solution.py:96
  363.8 1.1 multiply_reduce_fusion.1
  365.0 0.4 fusion
  365.4 0.4 fusion.116
  365.9 0.9 broadcast_multiply_fusion
  366.8 90.9 %all-reduce.16.cloned.1.call-done = f32[8,128,128]{2,1,0:T(8,128)} async-done(((f32[8,128,128]{2,1,0:T(8,128)}), f32[8,128,128]{2,1,0:T(8,128)}) %all-reduce.16.cloned.1.call-update) | async-done | bytes 524304 | tf_op jit(solution)/shard_map/psum | solution.py:96
  457.7 1.1 multiply_reduce_fusion
  459.1 11.7 %cholesky.55 = f32[128,128]{1,0:T(8,128)S(1)} custom-call(f32[128,128]{1,0:T(8,128)S(1)} %fusion.106), custom_call_target="Cholesky" | custom-call | tf_op jit(solution)/shard_map/jit(cholesky)/cholesky | solution.py:121
  470.9 0.6 compare_reduce_fusion
  471.5 0.7 fusion.104
  472.2 9.8 %custom-call.7 = f32[1,128,128]{1,2,0:T(8,128)S(1)} custom-call(f32[1,128,128]{2,1,0:T(8,128)S(1)} %fusion.104), custom_call_target="InvertDiagBlocksLowerTriangular" | custom-call | tf_op jit(solution)/shard_map/jit(_solve_triangular)/triangular_solve | solution.py:122
  482.0 0.3 convolution_convert_fusion.2
  482.3 0.4 convolution_convert_fusion
  482.6 0.1 pad_maximum_fusion
  482.8 1.6 copy.15
  (26 shorter events, 0.6 us)
Async XLA Ops:
  6.5 11.7 %copy-start = (bf16[6,8,64,256]{3,2,1,0:T(8,128)(2,1)S(1)}, bf16[6,8,64,256]{3,2,1,0:T(8,128)(2,1)}, u32[]{:S(2)}) copy-start(bf16[6,8,64,256]{3,2,1,0:T(8,128)(2,1)} %param.6) | copy-start | bytes 4718596
  6.5 6.5 %copy-start.2 = (s32[16]{0:T(128)S(1)}, s32[16]{0:T(128)}, u32[]{:S(2)}) copy-start(s32[16]{0:T(128)} %param.8) | copy-start | bytes 196
  6.5 9.5 %copy-start.1 = (f32[6,512]{1,0:T(8,128)S(1)}, f32[6,512]{1,0:T(8,128)}, u32[]{:S(2)}) copy-start(f32[6,512]{1,0:T(8,128)} %param.7) | copy-start | bytes 36868
  6.5 240.3 %all-reduce.12.cloned.1.call-start = ((), (), s32[]{:S(2)}) async-start(), calls=%async_computation | async-start | bytes 1048576 | tf_op jit(solution)/shard_map/psum | solution.py:96
  9.3 6.8 %collective-permute-start = (bf16[3,8,64,256]{3,2,1,0:T(8,128)(2,1)}, bf16[3,8,64,256]{3,2,1,0:T(8,128)(2,1)S(1)}, u32[]{:S(2)}, u32[]{:S(2)}) collective-permute-start(bf16[3,8,64,256]{3,2,1,0:T(8,128)(2,1)} %get-tuple-element.13), channel_id=1, source_target_pairs={{0,1},{1,2},{2,3},{3,4},{4,5},{5,6},{6,7},{7,8},{8,9},{9,10},{10,1... | collective-permute-start | bytes 2359304 | tf_op jit(solution)/shard_map/ppermute | solution.py:23
  11.7 6.5 %collective-permute-start.1 = (bf16[3,8,64,256]{3,2,1,0:T(8,128)(2,1)}, bf16[3,8,64,256]{3,2,1,0:T(8,128)(2,1)S(1)}, u32[]{:S(2)}, u32[]{:S(2)}) collective-permute-start(bf16[3,8,64,256]{3,2,1,0:T(8,128)(2,1)} %get-tuple-element.14), channel_id=1, source_target_pairs={{1,0},{2,1},{3,2},{4,3},{5,4},{6,5},{7,6},{8,7},{9,8},{10,9},{11,1... | collective-permute-start | bytes 2359304 | tf_op jit(solution)/shard_map/ppermute | solution.py:26
  25.9 17.6 %collective-permute-start.2 = (bf16[3,8,64,256]{3,2,1,0:T(8,128)(2,1)S(1)}, bf16[3,8,64,256]{3,2,1,0:T(8,128)(2,1)S(1)}, u32[]{:S(2)}, u32[]{:S(2)}) collective-permute-start(bf16[3,8,64,256]{3,2,1,0:T(8,128)(2,1)S(1)} %get-tuple-element.11), channel_id=1, source_target_pairs={{0,1},{1,2},{2,3},{3,4},{4,5},{5,6},{6,7},{7,8},{8,9},{9,10},{10,1... | collective-permute-start | bytes 2359304 | tf_op jit(solution)/shard_map/ppermute | solution.py:23
  41.7 6.0 %collective-permute-start.3 = (bf16[3,8,64,256]{3,2,1,0:T(8,128)(2,1)S(1)}, bf16[3,8,64,256]{3,2,1,0:T(8,128)(2,1)S(1)}, u32[]{:S(2)}, u32[]{:S(2)}) collective-permute-start(bf16[3,8,64,256]{3,2,1,0:T(8,128)(2,1)S(1)} %get-tuple-element.12), channel_id=1, source_target_pairs={{1,0},{2,1},{3,2},{4,3},{5,4},{6,5},{7,6},{8,7},{9,8},{10,9},{11,1... | collective-permute-start | bytes 2359304 | tf_op jit(solution)/shard_map/ppermute | solution.py:26
  69.5 17.5 %collective-permute-start.4 = (bf16[3,8,64,256]{3,2,1,0:T(8,128)(2,1)S(1)}, bf16[3,8,64,256]{3,2,1,0:T(8,128)(2,1)S(1)}, u32[]{:S(2)}, u32[]{:S(2)}) collective-permute-start(bf16[3,8,64,256]{3,2,1,0:T(8,128)(2,1)S(1)} %get-tuple-element.9), channel_id=1, source_target_pairs={{0,1},{1,2},{2,3},{3,4},{4,5},{5,6},{6,7},{7,8},{8,9},{9,10},{10,1... | collective-permute-start | bytes 2359304 | tf_op jit(solution)/shard_map/ppermute | solution.py:23
  85.1 6.1 %collective-permute-start.5 = (bf16[3,8,64,256]{3,2,1,0:T(8,128)(2,1)S(1)}, bf16[3,8,64,256]{3,2,1,0:T(8,128)(2,1)S(1)}, u32[]{:S(2)}, u32[]{:S(2)}) collective-permute-start(bf16[3,8,64,256]{3,2,1,0:T(8,128)(2,1)S(1)} %get-tuple-element.10), channel_id=1, source_target_pairs={{1,0},{2,1},{3,2},{4,3},{5,4},{6,5},{7,6},{8,7},{9,8},{10,9},{11,1... | collective-permute-start | bytes 2359304 | tf_op jit(solution)/shard_map/ppermute | solution.py:26
  113.0 17.5 %collective-permute-start.6 = (bf16[3,8,64,256]{3,2,1,0:T(8,128)(2,1)S(1)}, bf16[3,8,64,256]{3,2,1,0:T(8,128)(2,1)S(1)}, u32[]{:S(2)}, u32[]{:S(2)}) collective-permute-start(bf16[3,8,64,256]{3,2,1,0:T(8,128)(2,1)S(1)} %get-tuple-element.6), channel_id=1, source_target_pairs={{0,1},{1,2},{2,3},{3,4},{4,5},{5,6},{6,7},{7,8},{8,9},{9,10},{10,1... | collective-permute-start | bytes 2359304 | tf_op jit(solution)/shard_map/ppermute | solution.py:23
  128.6 6.1 %collective-permute-start.7 = (bf16[3,8,64,256]{3,2,1,0:T(8,128)(2,1)S(1)}, bf16[3,8,64,256]{3,2,1,0:T(8,128)(2,1)S(1)}, u32[]{:S(2)}, u32[]{:S(2)}) collective-permute-start(bf16[3,8,64,256]{3,2,1,0:T(8,128)(2,1)S(1)} %get-tuple-element.8), channel_id=1, source_target_pairs={{1,0},{2,1},{3,2},{4,3},{5,4},{6,5},{7,6},{8,7},{9,8},{10,9},{11,1... | collective-permute-start | bytes 2359304 | tf_op jit(solution)/shard_map/ppermute | solution.py:26
  143.9 219.8 %all-reduce.14.cloned.1.call-start = ((), (), s32[]{:S(2)}) async-start(), calls=%async_computation.1 | async-start | bytes 1048576 | tf_op jit(solution)/shard_map/psum | solution.py:96
  273.1 184.7 %all-reduce.16.cloned.1.call-start = ((), (), s32[]{:S(2)}) async-start(), calls=%async_computation.2 | async-start | bytes 1048576 | tf_op jit(solution)/shard_map/psum | solution.py:96
Sparse Core Ops, SparseCore 0:
  144.1 102.7 all-reduce.11
  273.2 90.5 all-reduce.13
  367.2 90.4 all-reduce.15
where the time goes:
time: 491 us
  waiting for transfers between devices  298 us (61%)
  other arithmetic  108 us (22%)
  starting transfers between devices  55 us (11%)
  between operations  16.5 us (3%)
  local copies, waits for them, and re-layouts  10.7 us (2%)
    psum x3, waiting for transfers between devices, domain_total(): summed = lax.psum(picker[:, None, None] * term[None], 'gz')  282 us
    ppermute x4, starting transfers between devices, extended_2(): lax.ppermute(lax.slice_in_dim(block, block.shape[dim] - width, None, axis...  49.3 us
    convert_element_type x3, other arithmetic, shards(): newer = (2.0 / EWIDTH * (image - CSHIFT * extended[3:-3]) - older.astype(...  44.4 us
    another operation x6, other arithmetic, shards(): factor = jnp.linalg.cholesky(gram)  24.8 us
    another operation x4, other arithmetic, shards(): inverse = jax.scipy.linalg.solve_triangular(factor, identity, lower=True)  20.9 us
    ppermute x4, waiting for transfers between devices, extended_2(): lax.ppermute(lax.slice_in_dim(block, 0, width, axis=dim), axis, backward)  14.7 us
  transfers between devices with their start and end apart: 11, of which 9 were waited for; matrix products, arithmetic and copies ran while one was open for 1% of the time, Pallas kernels for 0%

commit v1 on v0

v1 whole, which is shorter than its diff:
```python
import functools

import jax
import jax.numpy as jnp
import ml_dtypes
import numpy as np
from jax import lax
from jax.experimental import pallas as pl
from jax.experimental.pallas import tpu as pltpu
from jax.sharding import PartitionSpec as P

PANEL = 128
NX = 64
NY = 8
CELLS = NX * NY
DEGREE = 4
COEF = (-49.0 / 18.0, 1.5, -0.15, 1.0 / 90.0)
CSHIFT = 7.0
EWIDTH = 5.0
HALO = 3
TILE = 128
MESH = pl.DeviceIdType.MESH


def plane_matrix():
    full = np.zeros((CELLS, CELLS), np.float64)
    for y in range(NY):
        for x in range(NX):
            row = y * NX + x
            for k in (1, 2, 3):
                for s in (-k, k):
                    if 0 <= x + s < NX:
                        full[row, row + s] += -0.5 * COEF[k]
                    if 0 <= y + s < NY:
                        full[row, row + s * NX] += -0.5 * COEF[k]
    high = full.astype(ml_dtypes.bfloat16)
    low = (full - high.astype(np.float64)).astype(ml_dtypes.bfloat16)
    return np.stack([high, low])


def filter_kernel(
    n, rows, wav, pot, wz, wg, amat, fil_out, g_out,
    ext, last, potb, diag, fil, acc, gsend, grecv, gback, gfin,
    in_send, in_recv, pot_send, pot_recv, halo_send, halo_recv,
    out_send, out_recv, a_send, a_recv, b_send, b_recv,
):
    me = lax.axis_index("gz")
    planes = wav.shape[0]
    own = 2 * planes
    quad = me // 4
    r = me % 4
    half = r // 2
    core = r % 2
    link = quad * 2 + core
    lower_dev = ((link - 1) // 2) * 4 + 2 * half + (link + 1) % 2
    upper_dev = ((link + 1) // 2) * 4 + 2 * half + (link + 1) % 2
    has_lower = link > 0
    has_upper = link < n // 2 - 1

    barrier = pltpu.get_barrier_semaphore()

    @pl.loop(1, n)
    def _(off):
        pl.semaphore_signal(
            barrier, inc=1, device_id={"gz": (me + off) % n}, device_id_type=MESH
        )

    pl.semaphore_wait(barrier, n - 1)

    slot = r % 2
    starts = (HALO * slot, HALO * (1 - slot))

    def in_copy(h, piece, remote):
        start = starts[piece]
        src = wav.at[pl.ds(start, HALO), :, h * PANEL : (h + 1) * PANEL]
        dst = ext.at[0, pl.ds(HALO + planes * slot + start, HALO)]
        if remote:
            return pltpu.make_async_remote_copy(
                src_ref=src, dst_ref=dst,
                send_sem=in_send.at[h, piece], recv_sem=in_recv.at[slot, piece],
                device_id={"gz": quad * 4 + 2 * h + half}, device_id_type=MESH,
            )
        return pltpu.make_async_copy(src, dst, in_recv.at[slot, piece])

    def pot_copy(h, remote):
        if remote:
            return pltpu.make_async_remote_copy(
                src_ref=pot, dst_ref=potb.at[slot],
                send_sem=pot_send.at[h], recv_sem=pot_recv.at[slot],
                device_id={"gz": quad * 4 + 2 * h + half}, device_id_type=MESH,
            )
        return pltpu.make_async_copy(pot, potb.at[slot], pot_recv.at[slot])

    for h in (0, 1):
        away = quad * 4 + 2 * h + half != me

        @pl.when(away)
        def _(h=h):
            in_copy(h, 0, True).start()
            pot_copy(h, True).start()
            in_copy(h, 1, True).start()

        @pl.when(jnp.logical_not(away))
        def _(h=h):
            in_copy(h, 0, False).start()
            pot_copy(h, False).start()
            in_copy(h, 1, False).start()

    @pl.when(jnp.logical_not(has_lower))
    def _():
        for step in range(DEGREE):
            ext[step, 0:HALO] = jnp.zeros((HALO, CELLS, PANEL), jnp.bfloat16)

    @pl.when(jnp.logical_not(has_upper))
    def _():
        for step in range(DEGREE):
            ext[step, HALO + own : HALO + own + HALO] = jnp.zeros(
                (HALO, CELLS, PANEL), jnp.bfloat16
            )

    def in_wait(which, piece):
        start = HALO * which if piece == 0 else HALO * (1 - which)
        dst = ext.at[0, pl.ds(HALO + planes * which + start, HALO)]
        pltpu.make_async_copy(dst, dst, in_recv.at[which, piece]).wait()

    def down_copy(step):
        return pltpu.make_async_remote_copy(
            src_ref=ext.at[step, pl.ds(HALO, HALO)],
            dst_ref=ext.at[step, pl.ds(HALO + own, HALO)],
            send_sem=halo_send.at[step, 0], recv_sem=halo_recv.at[step, 0],
            device_id={"gz": lower_dev}, device_id_type=MESH,
        )

    def up_copy(step):
        return pltpu.make_async_remote_copy(
            src_ref=ext.at[step, pl.ds(own, HALO)],
            dst_ref=ext.at[step, pl.ds(0, HALO)],
            send_sem=halo_send.at[step, 1], recv_sem=halo_recv.at[step, 1],
            device_id={"gz": upper_dev}, device_id_type=MESH,
        )

    def send_halos(step):
        @pl.when(has_lower)
        def _():
            down_copy(step).start()

        @pl.when(has_upper)
        def _():
            up_copy(step).start()

    def wait_halos(step):
        @pl.when(has_upper)
        def _():
            down_copy(step).wait_recv()

        @pl.when(has_lower)
        def _():
            up_copy(step).wait_recv()

    in_wait(0, 0)
    in_wait(1, 0)
    send_halos(0)

    for which in (0, 1):
        pltpu.make_async_copy(potb.at[which], potb.at[which], pot_recv.at[which]).wait()

        @pl.loop(0, planes)
        def _(i, which=which):
            row = potb[which, pl.ds(i, 1), :] - (CSHIFT + 1.5 * COEF[0])
            diag[planes * which + i] = jnp.broadcast_to(row, (PANEL, CELLS)).T

    in_wait(0, 1)
    in_wait(1, 1)

    def update(step, first, second):
        pair = jnp.concatenate([ext[step, HALO + first], ext[step, HALO + second]], axis=1)
        for tile in range(CELLS // TILE):
            at = slice(tile * TILE, (tile + 1) * TILE)
            image = jnp.dot(
                amat[0, at, :], pair, preferred_element_type=jnp.float32
            ) + jnp.dot(amat[1, at, :], pair, preferred_element_type=jnp.float32)
            for place, plane in enumerate((first, second)):
                value = image[:, place * PANEL : (place + 1) * PANEL]
                centre = ext[step, HALO + plane, at, :].astype(jnp.float32)
                value = value + diag[plane, at, :] * centre
                for k in (1, 2, 3):
                    value = value + wz[plane, 2 * k - 2] * ext[
                        step, HALO + plane - k, at, :
                    ].astype(jnp.float32)
                    value = value + wz[plane, 2 * k - 1] * ext[
                        step, HALO + plane + k, at, :
                    ].astype(jnp.float32)
                if step == 0:
                    value = value * (1.0 / EWIDTH)
                else:
                    older = ext[step - 1, HALO + plane, at, :].astype(jnp.float32)
                    value = value * (2.0 / EWIDTH) - older
                value = value.astype(jnp.bfloat16)
                if step < DEGREE - 1:
                    ext[step + 1, HALO + plane, at, :] = value
                else:
                    last[plane, at, :] = value

    def out_copy(which, piece, remote):
        start = HALO * which if piece == 0 else HALO * (1 - which)
        src = last.at[pl.ds(planes * which + start, HALO)]
        dst = fil.at[half, pl.ds(start, HALO)]
        if remote:
            return pltpu.make_async_remote_copy(
                src_ref=src, dst_ref=dst,
                send_sem=out_send.at[which, piece], recv_sem=out_recv.at[half, piece],
                device_id={"gz": quad * 4 + 2 * core + which}, device_id_type=MESH,
            )
        return pltpu.make_async_copy(src, dst, out_recv.at[half, piece])

    def send_out(piece):
        for which in (0, 1):
            away = quad * 4 + 2 * core + which != me

            @pl.when(away)
            def _(which=which):
                out_copy(which, piece, True).start()

            @pl.when(jnp.logical_not(away))
            def _(which=which):
                out_copy(which, piece, False).start()

    for step in range(DEGREE):
        wait_halos(step)

        @pl.loop(0, HALO)
        def _(t, step=step):
            update(step, t, own - 1 - t)

        if step < DEGREE - 1:
            send_halos(step + 1)
        else:
            send_out(0)

        @pl.loop(0, HALO)
        def _(t, step=step):
            update(step, HALO + t, own - 1 - HALO - t)

    send_out(1)

    def out_wait(h, piece):
        start = HALO * slot if piece == 0 else HALO * (1 - slot)
        dst = fil.at[h, pl.ds(start, HALO)]
        pltpu.make_async_copy(dst, dst, out_recv.at[h, piece]).wait()

    for piece in (0, 1):
        for h in (0, 1):
            out_wait(h, piece)

    acc[...] = jnp.zeros_like(acc)

    @pl.loop(0, planes)
    def _(i):
        both = jnp.concatenate([fil[0, i], fil[1, i]], axis=1)
        fil_out[i] = both
        gram = lax.dot_general(
            both, both, (((0,), (0,)), ((), ())), preferred_element_type=jnp.float32
        )
        acc[0] += gram[0:PANEL, 0:PANEL]
        acc[1] += gram[0:PANEL, PANEL:]
        acc[2] += gram[PANEL:, PANEL:]

    @pl.loop(0, n)
    def _(j):
        at = pl.ds(pl.multiple_of(j * rows, rows), rows)
        gsend[j] = acc[:, at, :]

    def exchange(src, dst, send, recv):
        def copy(target, origin):
            return pltpu.make_async_remote_copy(
                src_ref=src.at[target], dst_ref=dst.at[origin],
                send_sem=send.at[target], recv_sem=recv.at[origin],
                device_id={"gz": target}, device_id_type=MESH,
            )

        @pl.loop(1, n)
        def _(off):
            copy((me + off) % n, me).start()

        dst[me] = src[me]

        @pl.loop(1, n)
        def _(off):
            copy((me + off) % n, (me + off) % n).wait_recv()

    exchange(gsend, grecv, a_send, a_recv)

    @pl.loop(0, n)
    def _(j):
        def add(i, total):
            return total + wg[j, i] * grecv[i]

        gback[j] = lax.fori_loop(0, n, add, jnp.zeros((3, rows, PANEL), jnp.float32))

    exchange(gback, gfin, b_send, b_recv)
    g_out[...] = gfin[...]

    for h in (0, 1):
        away = quad * 4 + 2 * h + half != me

        @pl.when(away)
        def _(h=h):
            in_copy(h, 0, True).wait_send()
            pot_copy(h, True).wait_send()
            in_copy(h, 1, True).wait_send()

        back = quad * 4 + 2 * core + h != me

        @pl.when(back)
        def _(h=h):
            out_copy(h, 0, True).wait_send()
            out_copy(h, 1, True).wait_send()

    for step in range(DEGREE):

        @pl.when(has_lower)
        def _(step=step):
            down_copy(step).wait_send()

        @pl.when(has_upper)
        def _(step=step):
            up_copy(step).wait_send()

    @pl.loop(1, n)
    def _(off):
        there = (me + off) % n
        pltpu.make_async_copy(gsend.at[there], gsend.at[there], a_send.at[there]).wait()
        pltpu.make_async_copy(gback.at[there], gback.at[there], b_send.at[there]).wait()


def filtered_and_gram(n, waves, potential, domain_of):
    planes = waves.shape[0]
    bands = waves.shape[2]
    rows = PANEL // n
    own = 2 * planes
    me = lax.axis_index("gz")
    base = 4 * (me // 4) + 2 * (me % 2)
    plane = jnp.arange(own)
    home = domain_of[base + plane // planes]
    columns = []
    for k in (1, 2, 3):
        for s in (-k, k):
            block = base + (plane + s + planes) // planes - 1
            inside = (block >= 0) & (block < n)
            linked = inside & (domain_of[jnp.clip(block, 0, n - 1)] == home)
            columns.append(jnp.where(linked, -0.5 * COEF[k], 0.0).astype(jnp.float32))
    wz = jnp.stack(columns, axis=1)
    same = (domain_of[:, None] == domain_of[None, :]).astype(jnp.float32)
    wg = same / (jnp.sum(same, axis=1, keepdims=True) * (planes * CELLS))
    vmem = pl.BlockSpec(memory_space=pltpu.VMEM)
    smem = pl.BlockSpec(memory_space=pltpu.SMEM)
    hbm = pl.BlockSpec(memory_space=pl.ANY)
    dma = pltpu.SemaphoreType.DMA
    chunk = pltpu.VMEM((n, 3, rows, PANEL), jnp.float32)
    return pl.pallas_call(
        functools.partial(filter_kernel, n, rows),
        out_shape=(
            jax.ShapeDtypeStruct((planes, CELLS, bands), jnp.bfloat16),
            jax.ShapeDtypeStruct((n, 3, rows, PANEL), jnp.float32),
        ),
        in_specs=[hbm, vmem, smem, smem, vmem],
        out_specs=(vmem, vmem),
        scratch_shapes=[
            pltpu.VMEM((DEGREE, own + 2 * HALO, CELLS, PANEL), jnp.bfloat16),
            pltpu.VMEM((own, CELLS, PANEL), jnp.bfloat16),
            pltpu.VMEM((2, planes, CELLS), jnp.float32),
            pltpu.VMEM((own, CELLS, PANEL), jnp.float32),
            pltpu.VMEM((2, planes, CELLS, PANEL), jnp.bfloat16),
            pltpu.VMEM((3, PANEL, PANEL), jnp.float32),
            chunk, chunk, chunk, chunk,
            dma((2, 2)), dma((2, 2)), dma((2,)), dma((2,)),
            dma((DEGREE, 2)), dma((DEGREE, 2)), dma((2, 2)), dma((2, 2)),
            dma((n,)), dma((n,)), dma((n,)), dma((n,)),
        ],
        compiler_params=pltpu.CompilerParams(
            collective_id=0, has_side_effects=True, vmem_limit_bytes=40 * 2**20
        ),
        cost_estimate=pl.CostEstimate(
            flops=8 * 10**9, bytes_accessed=5 * 10**6, transcendentals=0
        ),
        name="filter_gram",
    )(waves, potential, wz, wg, jnp.asarray(plane_matrix()))


def exact(a, b):
    return jnp.dot(a, b, precision=lax.Precision.HIGHEST, preferred_element_type=jnp.float32)


def whiten(gram):
    factor = jnp.linalg.cholesky(gram)
    inverse = jax.scipy.linalg.solve_triangular(
        factor, jnp.eye(PANEL, dtype=jnp.float32), lower=True
    )
    return inverse.T.astype(jnp.bfloat16)


def shards(waves, potential, domain_of):
    n = lax.axis_size("gz")
    planes = waves.shape[0]
    bands = waves.shape[3]
    filtered, sums = filtered_and_gram(
        n, waves.reshape(planes, CELLS, bands), potential, domain_of
    )
    sums = jnp.swapaxes(sums, 0, 1).reshape(3, PANEL, PANEL)
    g00, g01, g11 = sums[0], sums[1], sums[2]
    cells = filtered.reshape(planes * CELLS, bands)
    b0, b1 = cells[:, :PANEL], cells[:, PANEL:]
    w0 = whiten(g00)
    w0f = w0.astype(jnp.float32)
    corr = exact(w0f.T, g01)
    corr_r = corr.astype(jnp.bfloat16)
    cf = corr_r.astype(jnp.float32)
    cross = exact(cf.T, corr)
    gram1 = g11 - cross - cross.T + exact(cf.T, exact(exact(w0f.T, exact(g00, w0f)), cf))
    w1 = whiten(gram1)
    e0 = jnp.dot(b0, w0, preferred_element_type=jnp.float32).astype(jnp.bfloat16)
    reduced = (
        b1.astype(jnp.float32) - jnp.dot(e0, corr_r, preferred_element_type=jnp.float32)
    ).astype(jnp.bfloat16)
    e1 = jnp.dot(reduced, w1, preferred_element_type=jnp.float32).astype(jnp.bfloat16)
    return jnp.concatenate([e0, e1], axis=1).reshape(planes, NY, NX, bands)


def solution(mesh):
    return jax.shard_map(
        shards,
        mesh=mesh,
        in_specs=(P(("groups", "gz"), None, None, None), P(("groups", "gz"), None), P("groups")),
        out_specs=P(("groups", "gz"), None, None, None),
        check_vma=False,
    )
```

time: 491 us -> 148 us (0.30)
  waiting for transfers between devices: 298 us -> 0 us
  Pallas kernels: 0 us -> 86 us
  other arithmetic: 108 us -> 47.7 us
  starting transfers between devices: 55 us -> 0 us
  between operations: 16.5 us -> 0.28 us
    psum x3 -> x0, waiting for transfers between devices: 282 us -> none  [domain_total(): summed = lax.psum(picker[:, None, None] * term[None], 'gz')]
    pallas_call x0 -> x1, Pallas kernels: none -> 86 us  [filtered_and_gram(): pl.pallas_call(functools.partial(filter_kernel, n, rows), out_shape=(jax....]
    ppermute x8 -> x0, starting transfers between devices: 54.5 us -> none  [the longest x4 49.3 us: extended_2(): lax.ppermute(lax.slice_in_dim(block, block.shape[dim] - width, None, axis...]
    convert_element_type x5 -> x0, other arithmetic: 51.6 us -> none  [the longest x3 44.4 us: shards(): newer = (2.0 / EWIDTH * (image - CSHIFT * extended[3:-3]) - older.astype(...]
    ppermute x8 -> x0, waiting for transfers between devices: 15.8 us -> none  [the longest x4 14.7 us: extended_2(): lax.ppermute(lax.slice_in_dim(block, 0, width, axis=dim), axis, backward)]
    slice x8 -> x0, local copies, waits for them, and re-layouts: 7.91 us -> none  [the longest x4 4.61 us: hamiltonian(): inner = extended[3:-3]]
    gather x0 -> x7, local copies, waits for them, and re-layouts: none -> 6.71 us  [the longest x6 6.06 us: filtered_and_gram(): linked = inside & (domain_of[jnp.clip(block, 0, n - 1)] == home)]
    mul x7 -> x1, other arithmetic: 5.62 us -> 0.01 us  [filtered_and_gram(): wg = same / (jnp.sum(same, axis=1, keepdims=True) * (planes * CELLS))]
  transfers between devices with their start and end apart: 11 -> 0, of which waited for: 9 -> 0; matrix products, arithmetic and copies ran while one was open for 1% -> 0% of each run, Pallas kernels for 0% -> 0%
where the time goes in v1:
time: 148 us
  Pallas kernels  86 us (58%)
  other arithmetic  47.7 us (32%)
  local copies, waits for them, and re-layouts  10.6 us (7%)
  matrix products  2.91 us (2%)
    pallas_call x1, Pallas kernels, filtered_and_gram(): pl.pallas_call(functools.partial(filter_kernel, n, rows), out_shape=(jax....  86 us
    another operation x6, other arithmetic, whiten(): factor = jnp.linalg.cholesky(gram)  24.8 us
    another operation x4, other arithmetic, whiten(): jax.scipy.linalg.solve_triangular(factor, jnp.eye(PANEL, dtype=jnp.float3...  21.1 us
    gather x6, local copies, waits for them, and re-layouts, filtered_and_gram(): linked = inside & (domain_of[jnp.clip(block, 0, n - 1)] == home)  6.06 us

profile of v1, /device:TPU:0, one launch (start us, length us, event | category | flops | bytes accessed | tf_op | source)
XLA Modules:
  0.0 147.5 jit_solution(965336934014537605)
XLA Ops:
  0.0 0.0 copy-start.3
  0.0 0.9 convert_reduce_fusion
  1.0 0.1 fusion.40
  1.1 0.1 fusion.36
  1.2 0.1 fusion.38
  1.3 0.1 fusion.34
  1.5 1.3 gather_fusion
  2.8 0.0 copy-start
  2.8 0.0 copy-start.1
  2.8 1.4 gather_fusion.5
  4.3 1.3 gather_fusion.3
  5.6 0.0 copy-done.3
  5.6 0.7 gather_fusion.1
  6.3 0.7 gather_fusion.2
  6.9 0.7 gather_fusion.6
  7.6 0.7 gather_fusion.4
  8.3 0.1 copy.23
  8.4 0.1 copy.22
  8.5 0.1 copy.21
  8.6 0.1 copy.20
  8.7 0.1 copy.19
  8.8 0.1 copy.18
  9.1 0.1 stack.2.wz
  9.1 0.1 convert_divide_fusion.wg
  9.2 0.0 copy-done
  9.2 0.0 copy-done.1
  9.2 0.0 copy-start.2
  9.3 1.2 copy-done.2
  10.5 86.0 %filter_gram.1 = (bf16[6,512,256]{2,1,0:T(8,128)(2,1)S(1)}, f32[16,3,8,128]{3,2,1,0:T(8,128)S(1)}) custom-call(bf16[6,512,256]{2,1,0:T(8,128)(2,1)S(1)} %bitcast.64, f32[6,512]{1,0:T(8,128)S(1)} %copy-done.1, f32[12,6]{1,0:T(8,128)S(1)} %stack.2.wz, f32[16,16]{1,0:T(8,128)S(1)} %convert_divide_fusion.wg, bf16[2,512,512]{2,1,0:T(8,128)(2,1)S(1)} %copy-done.2), custom_call_target="tpu_custom_call" | custom-call | flops 8000000000 | bytes 5000000 | tf_op jit(solution)/shard_map/filter_gram/pallas_call | solution.py:360
  96.5 0.1 copy.25
  96.6 0.1 copy.24
  96.7 11.7 %cholesky.44 = f32[128,128]{1,0:T(8,128)S(1)} custom-call(f32[128,128]{1,0:T(8,128)S(1)} %fusion.11), custom_call_target="Cholesky" | custom-call | tf_op jit(solution)/shard_map/jit(cholesky)/cholesky | solution.py:395
  108.5 0.6 compare_reduce_fusion.1
  109.1 0.7 fusion.5
  109.8 9.8 %custom-call.6 = f32[1,128,128]{1,2,0:T(8,128)S(1)} custom-call(f32[1,128,128]{2,1,0:T(8,128)S(1)} %fusion.5), custom_call_target="InvertDiagBlocksLowerTriangular" | custom-call | tf_op jit(solution)/shard_map/jit(_solve_triangular)/triangular_solve | solution.py:396
  119.6 0.3 convolution_convert_fusion.3
  119.9 0.2 fusion.7
  120.1 0.2 fusion.48
  120.3 0.2 fusion.49
  120.5 0.2 fusion.13
  120.7 0.2 fusion.15
  120.9 0.1 copy.26
  121.0 0.3 convolution_add_fusion
  121.3 0.1 copy.28
  121.4 11.7 %cholesky.55 = f32[128,128]{1,0:T(8,128)S(1)} custom-call(f32[128,128]{1,0:T(8,128)S(1)} %fusion.9), custom_call_target="Cholesky" | custom-call | tf_op jit(solution)/shard_map/jit(cholesky)/cholesky | solution.py:395
  133.1 0.6 compare_reduce_fusion
  133.8 0.7 fusion.6
  134.4 10.0 %custom-call.7 = f32[1,128,128]{1,2,0:T(8,128)S(1)} custom-call(f32[1,128,128]{2,1,0:T(8,128)S(1)} %fusion.6), custom_call_target="InvertDiagBlocksLowerTriangular" | custom-call | tf_op jit(solution)/shard_map/jit(_solve_triangular)/triangular_solve | solution.py:396
  144.4 0.3 convolution_convert_fusion.2
  144.7 0.4 convolution_convert_fusion.1
  145.1 0.7 convolution_convert_fusion
  145.8 0.1 pad_maximum_fusion
  146.0 1.6 %copy.29 = bf16[3072,256]{1,0:T(8,128)(2,1)} copy(bf16[3072,256]{0,1:T(8,128)(2,1)S(1)} %pad_maximum_fusion) | data formatting | bytes 3145728 | tf_op jit(solution)/shard_map/concatenate | solution.py:426
  (20 shorter events, 0.3 us)
Async XLA Ops:
  0.0 5.6 %copy-start.3 = (s32[16]{0:T(128)S(1)}, s32[16]{0:T(128)}, u32[]{:S(2)}) copy-start(s32[16]{0:T(128)} %param.9) | copy-start | bytes 196
  2.8 6.4 %copy-start = (bf16[6,8,64,256]{3,2,1,0:T(8,128)(2,1)S(1)}, bf16[6,8,64,256]{3,2,1,0:T(8,128)(2,1)}, u32[]{:S(2)}) copy-start(bf16[6,8,64,256]{3,2,1,0:T(8,128)(2,1)} %param.7) | copy-start | bytes 4718596
  2.8 6.4 %copy-start.1 = (f32[6,512]{1,0:T(8,128)S(1)}, f32[6,512]{1,0:T(8,128)}, u32[]{:S(2)}) copy-start(f32[6,512]{1,0:T(8,128)} %pot.1) | copy-start | bytes 36868
  9.2 1.2 copy-start.2

commit v2 on v1

--- a/solution.py
+++ b/solution.py
@@ -18,6 +18,7 @@
 CSHIFT = 7.0
 EWIDTH = 5.0
 HALO = 3
+SCALE = 2.0 / EWIDTH
 TILE = 128
 MESH = pl.DeviceIdType.MESH
 
@@ -30,17 +31,17 @@
             for k in (1, 2, 3):
                 for s in (-k, k):
                     if 0 <= x + s < NX:
-                        full[row, row + s] += -0.5 * COEF[k]
+                        full[row, row + s] += -0.5 * SCALE * COEF[k]
                     if 0 <= y + s < NY:
-                        full[row, row + s * NX] += -0.5 * COEF[k]
+                        full[row, row + s * NX] += -0.5 * SCALE * COEF[k]
     high = full.astype(ml_dtypes.bfloat16)
     low = (full - high.astype(np.float64)).astype(ml_dtypes.bfloat16)
     return np.stack([high, low])
 
 
 def filter_kernel(
-    n, rows, wav, pot, wz, wg, amat, fil_out, g_out,
-    ext, last, potb, diag, fil, acc, gsend, grecv, gback, gfin,
+    n, rows, dom, wav, pot, amat, fil_out, g_out,
+    wz, ext, last, potb, diag, fil, acc, gsend, grecv, gback, gfin,
     in_send, in_recv, pot_send, pot_recv, halo_send, halo_recv,
     out_send, out_recv, a_send, a_recv, b_send, b_recv,
 ):
@@ -67,6 +68,20 @@
 
     pl.semaphore_wait(barrier, n - 1)
 
+    first = quad * 4 + core * 2
+    marks = [dom[jnp.clip(first + b, 0, n - 1)] for b in (-1, 0, 1, 2)]
+    ones = [
+        jnp.where((marks[0] == marks[1]) & has_lower, 1.0, 0.0).astype(jnp.float32),
+        jnp.where(marks[1] == marks[2], 1.0, 0.0).astype(jnp.float32),
+        jnp.where((marks[2] == marks[3]) & has_upper, 1.0, 0.0).astype(jnp.float32),
+    ]
+    for plane in range(own):
+        for k in (1, 2, 3):
+            for place, other in enumerate((plane - k, plane + k)):
+                a, b = plane // planes, other // planes
+                weight = -0.5 * SCALE * COEF[k]
+                wz[plane, 2 * k - 2 + place] = ones[max(a, b)] * weight if a != b else weight
+
     slot = r % 2
     starts = (HALO * slot, HALO * (1 - slot))
 
@@ -166,7 +181,7 @@
 
         @pl.loop(0, planes)
         def _(i, which=which):
-            row = potb[which, pl.ds(i, 1), :] - (CSHIFT + 1.5 * COEF[0])
+            row = SCALE * (potb[which, pl.ds(i, 1), :] - (CSHIFT + 1.5 * COEF[0]))
             diag[planes * which + i] = jnp.broadcast_to(row, (PANEL, CELLS)).T
 
     in_wait(0, 1)
@@ -191,10 +206,10 @@
                         step, HALO + plane + k, at, :
                     ].astype(jnp.float32)
                 if step == 0:
-                    value = value * (1.0 / EWIDTH)
+                    value = value * 0.5
                 else:
                     older = ext[step - 1, HALO + plane, at, :].astype(jnp.float32)
-                    value = value * (2.0 / EWIDTH) - older
+                    value = value - older
                 value = value.astype(jnp.bfloat16)
                 if step < DEGREE - 1:
                     ext[step + 1, HALO + plane, at, :] = value
@@ -292,13 +307,23 @@
 
     @pl.loop(0, n)
     def _(j):
-        def add(i, total):
-            return total + wg[j, i] * grecv[i]
-
-        gback[j] = lax.fori_loop(0, n, add, jnp.zeros((3, rows, PANEL), jnp.float32))
+        mark = dom[j]
+
+        def add(i, sums):
+            total, blocks = sums
+            same = jnp.where(dom[i] == mark, 1.0, 0.0).astype(jnp.float32)
+            return total + same * grecv[i], blocks + same
+
+        zero = jnp.zeros((3, rows, PANEL), jnp.float32)
+        total, blocks = lax.fori_loop(0, n, add, (zero, jnp.float32(0.0)), unroll=8)
+        size = jnp.full((3, rows, PANEL), blocks * (planes * CELLS), jnp.float32)
+        gback[j] = total / size
 
     exchange(gback, gfin, b_send, b_recv)
-    g_out[...] = gfin[...]
+
+    @pl.loop(0, n)
+    def _(j):
+        g_out[:, pl.ds(pl.multiple_of(j * rows, rows), rows), :] = gfin[j]
 
     for h in (0, 1):
         away = quad * 4 + 2 * h + half != me
@@ -338,20 +363,6 @@
     bands = waves.shape[2]
     rows = PANEL // n
     own = 2 * planes
-    me = lax.axis_index("gz")
-    base = 4 * (me // 4) + 2 * (me % 2)
-    plane = jnp.arange(own)
-    home = domain_of[base + plane // planes]
-    columns = []
-    for k in (1, 2, 3):
-        for s in (-k, k):
-            block = base + (plane + s + planes) // planes - 1
-            inside = (block >= 0) & (block < n)
-            linked = inside & (domain_of[jnp.clip(block, 0, n - 1)] == home)
-            columns.append(jnp.where(linked, -0.5 * COEF[k], 0.0).astype(jnp.float32))
-    wz = jnp.stack(columns, axis=1)
-    same = (domain_of[:, None] == domain_of[None, :]).astype(jnp.float32)
-    wg = same / (jnp.sum(same, axis=1, keepdims=True) * (planes * CELLS))
     vmem = pl.BlockSpec(memory_space=pltpu.VMEM)
     smem = pl.BlockSpec(memory_space=pltpu.SMEM)
     hbm = pl.BlockSpec(memory_space=pl.ANY)
@@ -361,11 +372,12 @@
         functools.partial(filter_kernel, n, rows),
         out_shape=(
             jax.ShapeDtypeStruct((planes, CELLS, bands), jnp.bfloat16),
-            jax.ShapeDtypeStruct((n, 3, rows, PANEL), jnp.float32),
+            jax.ShapeDtypeStruct((3, PANEL, PANEL), jnp.float32),
         ),
-        in_specs=[hbm, vmem, smem, smem, vmem],
+        in_specs=[smem, hbm, vmem, vmem],
         out_specs=(vmem, vmem),
         scratch_shapes=[
+            pltpu.SMEM((own, 6), jnp.float32),
             pltpu.VMEM((DEGREE, own + 2 * HALO, CELLS, PANEL), jnp.bfloat16),
             pltpu.VMEM((own, CELLS, PANEL), jnp.bfloat16),
             pltpu.VMEM((2, planes, CELLS), jnp.float32),
@@ -384,19 +396,77 @@
             flops=8 * 10**9, bytes_accessed=5 * 10**6, transcendentals=0
         ),
         name="filter_gram",
-    )(waves, potential, wz, wg, jnp.asarray(plane_matrix()))
-
-
-def exact(a, b):
-    return jnp.dot(a, b, precision=lax.Precision.HIGHEST, preferred_element_type=jnp.float32)
-
-
-def whiten(gram):
-    factor = jnp.linalg.cholesky(gram)
-    inverse = jax.scipy.linalg.solve_triangular(
-        factor, jnp.eye(PANEL, dtype=jnp.float32), lower=True
+    )(domain_of, waves, potential, jnp.asarray(plane_matrix()))
+
+
+BLOCK = 8
+
+
+def exact(a, b, contract=((1,), (0,))):
+    return lax.dot_general(
+        a, b, (contract, ((), ())),
+        precision=lax.Precision.HIGHEST, preferred_element_type=jnp.float32,
     )
-    return inverse.T.astype(jnp.bfloat16)
+
+
+def inverse_factor(gram):
+    row = lax.broadcasted_iota(jnp.int32, (BLOCK, PANEL), 0)
+    lane = lax.broadcasted_iota(jnp.int32, (BLOCK, PANEL), 1)
+    rest = gram
+    result = []
+    for start in range(0, PANEL, BLOCK):
+        top = rest[:BLOCK]
+        inside = (lane >= start) & (lane < start + BLOCK)
+        pivot_columns = [
+            jnp.broadcast_to(top[:, start + j : start + j + 1], (BLOCK, PANEL))
+            for j in range(BLOCK)
+        ]
+        top = jnp.where(inside, jnp.where(lane - start == row, 1.0, 0.0), top)
+        scale = jnp.zeros((BLOCK, PANEL), jnp.float32)
+        for j in range(BLOCK):
+            pivot = jnp.broadcast_to(pivot_columns[j][j : j + 1], (BLOCK, PANEL))
+            over = 1.0 / pivot
+            scale = jnp.where(row == j, over, scale)
+            if j == BLOCK - 1:
+                break
+            factor = jnp.where(row > j, pivot_columns[j] * over, 0.0)
+            for later in range(j + 1, BLOCK):
+                pivot_columns[later] = pivot_columns[later] - factor * jnp.broadcast_to(
+                    pivot_columns[later][j : j + 1], (BLOCK, PANEL)
+                )
+            top = top - factor * jnp.broadcast_to(top[j : j + 1], (BLOCK, PANEL))
+        end = start + BLOCK
+        result.append(jnp.where(lane < end, top * jnp.sqrt(scale), 0.0))
+        if end < PANEL:
+            ratio = jnp.where(lane >= end, top * scale, 0.0)
+            change = exact(ratio, top, ((0,), (0,)))[end:]
+            below = lax.broadcasted_iota(jnp.int32, (PANEL - end, PANEL), 1)
+            keep = jnp.where((below >= start) & (below < end), 0.0, rest[BLOCK:])
+            rest = keep - change
+    return jnp.concatenate(result, axis=0)
+
+
+def whiten_kernel(fil, sums, out):
+    g00, g01, g11 = sums[0], sums[1], sums[2]
+    w0 = inverse_factor(g00).astype(jnp.bfloat16)
+    w0f = w0.astype(jnp.float32)
+    corr = exact(w0f, g01)
+    corr_r = corr.astype(jnp.bfloat16)
+    cf = corr_r.astype(jnp.float32)
+    middle = exact(exact(exact(w0f, g00), w0f, ((1,), (1,))), cf) - corr
+    gram1 = g11 + exact(cf, middle, ((0,), (0,))) - exact(corr, cf, ((0,), (0,)))
+    w1 = inverse_factor(gram1).astype(jnp.bfloat16)
+
+    def times(a, b, contract):
+        return lax.dot_general(a, b, (contract, ((), ())), preferred_element_type=jnp.float32)
+
+    @pl.loop(0, fil.shape[0])
+    def _(i):
+        e0 = times(fil[i, :, :PANEL], w0, ((1,), (1,))).astype(jnp.bfloat16)
+        out[i, :, :PANEL] = e0
+        b1 = fil[i, :, PANEL:].astype(jnp.float32)
+        reduced = (b1 - times(e0, corr_r, ((1,), (0,)))).astype(jnp.bfloat16)
+        out[i, :, PANEL:] = times(reduced, w1, ((1,), (1,))).astype(jnp.bfloat16)
 
 
 def shards(waves, potential, domain_of):
@@ -406,24 +476,19 @@
     filtered, sums = filtered_and_gram(
         n, waves.reshape(planes, CELLS, bands), potential, domain_of
     )
-    sums = jnp.swapaxes(sums, 0, 1).reshape(3, PANEL, PANEL)
-    g00, g01, g11 = sums[0], sums[1], sums[2]
-    cells = filtered.reshape(planes * CELLS, bands)
-    b0, b1 = cells[:, :PANEL], cells[:, PANEL:]
-    w0 = whiten(g00)
-    w0f = w0.astype(jnp.float32)
-    corr = exact(w0f.T, g01)
-    corr_r = corr.astype(jnp.bfloat16)
-    cf = corr_r.astype(jnp.float32)
-    cross = exact(cf.T, corr)
-    gram1 = g11 - cross - cross.T + exact(cf.T, exact(exact(w0f.T, exact(g00, w0f)), cf))
-    w1 = whiten(gram1)
-    e0 = jnp.dot(b0, w0, preferred_element_type=jnp.float32).astype(jnp.bfloat16)
-    reduced = (
-        b1.astype(jnp.float32) - jnp.dot(e0, corr_r, preferred_element_type=jnp.float32)
-    ).astype(jnp.bfloat16)
-    e1 = jnp.dot(reduced, w1, preferred_element_type=jnp.float32).astype(jnp.bfloat16)
-    return jnp.concatenate([e0, e1], axis=1).reshape(planes, NY, NX, bands)
+    vmem = pl.BlockSpec(memory_space=pltpu.VMEM)
+    orbitals = pl.pallas_call(
+        whiten_kernel,
+        out_shape=jax.ShapeDtypeStruct((planes, CELLS, bands), jnp.bfloat16),
+        in_specs=[vmem, vmem],
+        out_specs=vmem,
+        compiler_params=pltpu.CompilerParams(vmem_limit_bytes=32 * 2**20),
+        cost_estimate=pl.CostEstimate(
+            flops=4 * 10**8, bytes_accessed=4 * 10**6, transcendentals=0
+        ),
+        name="whiten",
+    )(filtered, sums)
+    return orbitals.reshape(planes, NY, NX, bands)
 
 
 def solution(mesh):

time: 148 us -> 108 us (0.73)
  other arithmetic: 47.7 us -> 0 us
  Pallas kernels: 86 us -> 104 us
  local copies, waits for them, and re-layouts: 10.6 us -> 4 us
  matrix products: 2.91 us -> 0 us
    another operation x10 -> x0, other arithmetic: 45.9 us -> none  [the longest x6 24.8 us: whiten(): factor = jnp.linalg.cholesky(gram)]
    pallas_call x0 -> x1, Pallas kernels: none -> 19.5 us  [shards(): pl.pallas_call(whiten_kernel, out_shape=jax.ShapeDtypeStruct((planes, CEL...]
    gather x7 -> x0, local copies, waits for them, and re-layouts: 6.71 us -> none  [the longest x6 6.06 us: filtered_and_gram(): linked = inside & (domain_of[jnp.clip(block, 0, n - 1)] == home)]
    unnamed x8, local copies, waits for them, and re-layouts: 1.24 us -> 4 us
    dot_general x8 -> x0, matrix products: 2.34 us -> none  [the longest x6 1.23 us: exact(): jnp.dot(a, b, precision=lax.Precision.HIGHEST, preferred_element_type=jnp...]
    pallas_call x1, Pallas kernels: 86 us -> 84.3 us  [filtered_and_gram(): pl.pallas_call(functools.partial(filter_kernel, n, rows), out_shape=(jax....]
    concatenate x1 -> x0, local copies, waits for them, and re-layouts: 1.57 us -> none  [shards(): return jnp.concatenate([e0, e1], axis=1).reshape(planes, NY, NX, bands)]
where the time goes in v2:
time: 108 us
  Pallas kernels  104 us (96%)
  local copies, waits for them, and re-layouts  4 us (4%)
    pallas_call x1, Pallas kernels, filtered_and_gram(): pl.pallas_call(functools.partial(filter_kernel, n, rows), out_shape=(jax....  84.3 us
    pallas_call x1, Pallas kernels, shards(): pl.pallas_call(whiten_kernel, out_shape=jax.ShapeDtypeStruct((planes, CEL...  19.5 us
    unnamed x8, local copies, waits for them, and re-layouts  4 us

profile of v2, /device:TPU:0, one launch (start us, length us, event | category | flops | bytes accessed | tf_op | source)
XLA Modules:
  0.0 107.8 jit_solution(12254481360709283162)
XLA Ops:
  0.0 0.0 copy-start
  0.0 1.4 %copy-done = bf16[6,8,64,256]{3,2,1,0:T(8,128)(2,1)S(1)} copy-done((bf16[6,8,64,256]{3,2,1,0:T(8,128)(2,1)S(1)}, bf16[6,8,64,256]{3,2,1,0:T(8,128)(2,1)}, u32[]{:S(2)}) %copy-start) | copy-done | bytes 1572888
  1.4 0.0 copy-start.1
  1.4 0.7 copy-done.1
  2.1 0.0 copy-start.2
  2.1 0.7 copy-done.2
  2.8 0.0 copy-start.3
  2.8 1.2 %copy-done.3 = bf16[2,512,512]{2,1,0:T(8,128)(2,1)S(1)} copy-done((bf16[2,512,512]{2,1,0:T(8,128)(2,1)S(1)}, bf16[2,512,512]{2,1,0:T(8,128)(2,1)}, u32[]{:S(2)}) %copy-start.3) | copy-done | bytes 1048600
  4.0 84.3 %filter_gram.1 = (bf16[6,512,256]{2,1,0:T(8,128)(2,1)S(1)}, f32[3,128,128]{2,1,0:T(8,128)S(1)}) custom-call(s32[16]{0:T(128)S(1)} %copy-done.2, bf16[6,512,256]{2,1,0:T(8,128)(2,1)S(1)} %bitcast.2, f32[6,512]{1,0:T(8,128)S(1)} %copy-done.1, bf16[2,512,512]{2,1,0:T(8,128)(2,1)S(1)} %copy-done.3), custom_call_target="tpu_custom_call" | custom-call | flops 8000000000 | bytes 5000000 | tf_op jit(solution)/shard_map/filter_gram/pallas_call | solution.py:371
  88.3 19.5 %whiten.1 = bf16[6,512,256]{2,1,0:T(8,128)(2,1)} custom-call(bf16[6,512,256]{2,1,0:T(8,128)(2,1)S(1)} %get-tuple-element.7.fil, f32[3,128,128]{2,1,0:T(8,128)S(1)} %get-tuple-element.8.sums), custom_call_target="tpu_custom_call" | custom-call | flops 400000000 | bytes 4000000 | tf_op jit(solution)/shard_map/whiten/pallas_call | solution.py:480
Async XLA Ops:
  0.0 1.4 %copy-start = (bf16[6,8,64,256]{3,2,1,0:T(8,128)(2,1)S(1)}, bf16[6,8,64,256]{3,2,1,0:T(8,128)(2,1)}, u32[]{:S(2)}) copy-start(bf16[6,8,64,256]{3,2,1,0:T(8,128)(2,1)} %param.4) | copy-start | bytes 4718596
  1.4 0.7 copy-start.1
  2.1 0.7 copy-start.2
  2.8 1.2 %copy-start.3 = (bf16[2,512,512]{2,1,0:T(8,128)(2,1)S(1)}, bf16[2,512,512]{2,1,0:T(8,128)(2,1)}, u32[]{:S(2)}) copy-start(bf16[2,512,512]{2,1,0:T(8,128)(2,1)} %constant.2.clone.amat) | copy-start | bytes 3145732

commit v3 on v2

--- a/solution.py
+++ b/solution.py
@@ -36,14 +36,15 @@
                         full[row, row + s * NX] += -0.5 * SCALE * COEF[k]
     high = full.astype(ml_dtypes.bfloat16)
     low = (full - high.astype(np.float64)).astype(ml_dtypes.bfloat16)
-    return np.stack([high, low])
+    tiles = np.stack([high, low]).reshape(2, CELLS // TILE, TILE, CELLS)
+    return np.swapaxes(tiles, 0, 1).reshape(CELLS // TILE, 2 * TILE, CELLS)
 
 
 def filter_kernel(
-    n, rows, dom, wav, pot, amat, fil_out, g_out,
-    wz, ext, last, potb, diag, fil, acc, gsend, grecv, gback, gfin,
+    n, rows, dom, wav, pot, amat_hbm, fil_out, g_out,
+    wz, amat, ext, last, potb, diag, fil, acc, gsend, grecv, gback, gfin,
     in_send, in_recv, pot_send, pot_recv, halo_send, halo_recv,
-    out_send, out_recv, a_send, a_recv, b_send, b_recv,
+    out_send, out_recv, load, store, a_send, a_recv, b_send, b_recv,
 ):
     me = lax.axis_index("gz")
     planes = wav.shape[0]
@@ -106,6 +107,7 @@
             )
         return pltpu.make_async_copy(pot, potb.at[slot], pot_recv.at[slot])
 
+    amat_copy = pltpu.make_async_copy(amat_hbm, amat, load)
     for h in (0, 1):
         away = quad * 4 + 2 * h + half != me
 
@@ -120,6 +122,8 @@
             in_copy(h, 0, False).start()
             pot_copy(h, False).start()
             in_copy(h, 1, False).start()
+
+    amat_copy.start()
 
     @pl.when(jnp.logical_not(has_lower))
     def _():
@@ -154,27 +158,47 @@
             device_id={"gz": upper_dev}, device_id_type=MESH,
         )
 
-    def send_halos(step):
-        @pl.when(has_lower)
+    def send_far(step):
+        @pl.when((core == 0) & has_lower)
         def _():
             down_copy(step).start()
 
-        @pl.when(has_upper)
+        @pl.when((core == 1) & has_upper)
         def _():
             up_copy(step).start()
 
-    def wait_halos(step):
-        @pl.when(has_upper)
+    def send_near(step):
+        @pl.when(core == 0)
+        def _():
+            up_copy(step).start()
+
+        @pl.when(core == 1)
+        def _():
+            down_copy(step).start()
+
+    def wait_far(step):
+        @pl.when((core == 0) & has_lower)
+        def _():
+            up_copy(step).wait_recv()
+
+        @pl.when((core == 1) & has_upper)
         def _():
             down_copy(step).wait_recv()
 
-        @pl.when(has_lower)
+    def wait_near(step):
+        @pl.when(core == 0)
+        def _():
+            down_copy(step).wait_recv()
+
+        @pl.when(core == 1)
         def _():
             up_copy(step).wait_recv()
 
-    in_wait(0, 0)
-    in_wait(1, 0)
-    send_halos(0)
+    in_wait(core, 0)
+    send_far(0)
+    in_wait(1 - core, 0)
+    send_near(0)
+    amat_copy.wait()
 
     for which in (0, 1):
         pltpu.make_async_copy(potb.at[which], potb.at[which], pot_recv.at[which]).wait()
@@ -191,9 +215,8 @@
         pair = jnp.concatenate([ext[step, HALO + first], ext[step, HALO + second]], axis=1)
         for tile in range(CELLS // TILE):
             at = slice(tile * TILE, (tile + 1) * TILE)
-            image = jnp.dot(
-                amat[0, at, :], pair, preferred_element_type=jnp.float32
-            ) + jnp.dot(amat[1, at, :], pair, preferred_element_type=jnp.float32)
+            both = jnp.dot(amat[tile], pair, preferred_element_type=jnp.float32)
+            image = both[:TILE] + both[TILE:]
             for place, plane in enumerate((first, second)):
                 value = image[:, place * PANEL : (place + 1) * PANEL]
                 centre = ext[step, HALO + plane, at, :].astype(jnp.float32)
@@ -216,69 +239,84 @@
                 else:
                     last[plane, at, :] = value
 
-    def out_copy(which, piece, remote):
-        start = HALO * which if piece == 0 else HALO * (1 - which)
-        src = last.at[pl.ds(planes * which + start, HALO)]
-        dst = fil.at[half, pl.ds(start, HALO)]
+    def out_copy(part, remote):
+        which, piece = part // 2, part % 2
+        src = last.at[pl.ds(HALO * part, HALO)]
+        dst = fil.at[half, pl.ds(HALO * piece, HALO)]
         if remote:
             return pltpu.make_async_remote_copy(
                 src_ref=src, dst_ref=dst,
-                send_sem=out_send.at[which, piece], recv_sem=out_recv.at[half, piece],
+                send_sem=out_send.at[part], recv_sem=out_recv.at[half, piece],
                 device_id={"gz": quad * 4 + 2 * core + which}, device_id_type=MESH,
             )
         return pltpu.make_async_copy(src, dst, out_recv.at[half, piece])
 
-    def send_out(piece):
-        for which in (0, 1):
-            away = quad * 4 + 2 * core + which != me
-
-            @pl.when(away)
-            def _(which=which):
-                out_copy(which, piece, True).start()
-
-            @pl.when(jnp.logical_not(away))
-            def _(which=which):
-                out_copy(which, piece, False).start()
+    def send_out(t_part):
+        part = jnp.where(core == 0, t_part, 3 - t_part)
+        away = quad * 4 + 2 * core + part // 2 != me
+
+        @pl.when(away)
+        def _():
+            out_copy(part, True).start()
+
+        @pl.when(jnp.logical_not(away))
+        def _():
+            out_copy(part, False).start()
+
+    def inward(t):
+        return jnp.where(core == 0, t, own - 1 - t)
+
+    def update_pairs(step, start, count):
+        @pl.loop(0, count)
+        def _(j):
+            update(step, inward(start + 2 * j), inward(start + 2 * j + 1))
 
     for step in range(DEGREE):
-        wait_halos(step)
-
-        @pl.loop(0, HALO)
-        def _(t, step=step):
-            update(step, t, own - 1 - t)
-
-        if step < DEGREE - 1:
-            send_halos(step + 1)
+        final = step == DEGREE - 1
+        wait_near(step)
+        update_pairs(step, own - 4, 2)
+        if final:
+            send_out(3)
         else:
+            send_near(step + 1)
+        update_pairs(step, own - 8, 2)
+        if final:
+            send_out(2)
+        wait_far(step)
+        update_pairs(step, 0, 2)
+        if final:
             send_out(0)
-
-        @pl.loop(0, HALO)
-        def _(t, step=step):
-            update(step, HALO + t, own - 1 - HALO - t)
-
-    send_out(1)
+            send_out(1)
+        else:
+            send_far(step + 1)
 
     def out_wait(h, piece):
-        start = HALO * slot if piece == 0 else HALO * (1 - slot)
-        dst = fil.at[h, pl.ds(start, HALO)]
+        dst = fil.at[h, pl.ds(HALO * piece, HALO)]
         pltpu.make_async_copy(dst, dst, out_recv.at[h, piece]).wait()
 
-    for piece in (0, 1):
+    def store_copy(h, piece):
+        return pltpu.make_async_copy(
+            fil.at[h, pl.ds(HALO * piece, HALO)],
+            fil_out.at[pl.ds(HALO * piece, HALO), :, h * PANEL : (h + 1) * PANEL],
+            store.at[h, piece],
+        )
+
+    acc[...] = jnp.zeros_like(acc)
+    for piece in (1 - half, half):
         for h in (0, 1):
             out_wait(h, piece)
-
-    acc[...] = jnp.zeros_like(acc)
-
-    @pl.loop(0, planes)
-    def _(i):
-        both = jnp.concatenate([fil[0, i], fil[1, i]], axis=1)
-        fil_out[i] = both
-        gram = lax.dot_general(
-            both, both, (((0,), (0,)), ((), ())), preferred_element_type=jnp.float32
-        )
-        acc[0] += gram[0:PANEL, 0:PANEL]
-        acc[1] += gram[0:PANEL, PANEL:]
-        acc[2] += gram[PANEL:, PANEL:]
+            store_copy(h, piece).start()
+
+        @pl.loop(0, HALO)
+        def _(i, piece=piece):
+            at = HALO * piece + i
+            both = jnp.concatenate([fil[0, at], fil[1, at]], axis=1)
+            gram = lax.dot_general(
+                both, both, (((0,), (0,)), ((), ())), preferred_element_type=jnp.float32
+            )
+            acc[0] += gram[0:PANEL, 0:PANEL]
+            acc[1] += gram[0:PANEL, PANEL:]
+            acc[2] += gram[PANEL:, PANEL:]
 
     @pl.loop(0, n)
     def _(j):
@@ -338,8 +376,11 @@
 
         @pl.when(back)
         def _(h=h):
-            out_copy(h, 0, True).wait_send()
-            out_copy(h, 1, True).wait_send()
+            out_copy(2 * h, True).wait_send()
+            out_copy(2 * h + 1, True).wait_send()
+
+        store_copy(h, 0).wait()
+        store_copy(h, 1).wait()
 
     for step in range(DEGREE):
 
@@ -374,10 +415,11 @@
             jax.ShapeDtypeStruct((planes, CELLS, bands), jnp.bfloat16),
             jax.ShapeDtypeStruct((3, PANEL, PANEL), jnp.float32),
         ),
-        in_specs=[smem, hbm, vmem, vmem],
-        out_specs=(vmem, vmem),
+        in_specs=[smem, hbm, hbm, hbm],
+        out_specs=(hbm, vmem),
         scratch_shapes=[
             pltpu.SMEM((own, 6), jnp.float32),
+            pltpu.VMEM((CELLS // TILE, 2 * TILE, CELLS), jnp.bfloat16),
             pltpu.VMEM((DEGREE, own + 2 * HALO, CELLS, PANEL), jnp.bfloat16),
             pltpu.VMEM((own, CELLS, PANEL), jnp.bfloat16),
             pltpu.VMEM((2, planes, CELLS), jnp.float32),
@@ -386,11 +428,11 @@
             pltpu.VMEM((3, PANEL, PANEL), jnp.float32),
             chunk, chunk, chunk, chunk,
             dma((2, 2)), dma((2, 2)), dma((2,)), dma((2,)),
-            dma((DEGREE, 2)), dma((DEGREE, 2)), dma((2, 2)), dma((2, 2)),
+            dma((DEGREE, 2)), dma((DEGREE, 2)), dma((4,)), dma((2, 2)), dma, dma((2, 2)),
             dma((n,)), dma((n,)), dma((n,)), dma((n,)),
         ],
         compiler_params=pltpu.CompilerParams(
-            collective_id=0, has_side_effects=True, vmem_limit_bytes=40 * 2**20
+            collective_id=0, has_side_effects=True, vmem_limit_bytes=58 * 2**20
         ),
         cost_estimate=pl.CostEstimate(
             flops=8 * 10**9, bytes_accessed=5 * 10**6, transcendentals=0
@@ -446,7 +488,9 @@
     return jnp.concatenate(result, axis=0)
 
 
-def whiten_kernel(fil, sums, out):
+def whiten_kernel(fil_hbm, sums, out_hbm, fil, out, load, store):
+    load_copy = pltpu.make_async_copy(fil_hbm, fil, load)
+    load_copy.start()
     g00, g01, g11 = sums[0], sums[1], sums[2]
     w0 = inverse_factor(g00).astype(jnp.bfloat16)
     w0f = w0.astype(jnp.float32)
@@ -460,6 +504,8 @@
     def times(a, b, contract):
         return lax.dot_general(a, b, (contract, ((), ())), preferred_element_type=jnp.float32)
 
+    load_copy.wait()
+
     @pl.loop(0, fil.shape[0])
     def _(i):
         e0 = times(fil[i, :, :PANEL], w0, ((1,), (1,))).astype(jnp.bfloat16)
@@ -467,6 +513,11 @@
         b1 = fil[i, :, PANEL:].astype(jnp.float32)
         reduced = (b1 - times(e0, corr_r, ((1,), (0,)))).astype(jnp.bfloat16)
         out[i, :, PANEL:] = times(reduced, w1, ((1,), (1,))).astype(jnp.bfloat16)
+        pltpu.make_async_copy(out.at[i], out_hbm.at[i], store.at[i]).start()
+
+    @pl.loop(0, fil.shape[0])
+    def _(i):
+        pltpu.make_async_copy(out.at[i], out_hbm.at[i], store.at[i]).wait()
 
 
 def shards(waves, potential, domain_of):
@@ -477,12 +528,19 @@
         n, waves.reshape(planes, CELLS, bands), potential, domain_of
     )
     vmem = pl.BlockSpec(memory_space=pltpu.VMEM)
+    hbm = pl.BlockSpec(memory_space=pl.ANY)
     orbitals = pl.pallas_call(
         whiten_kernel,
         out_shape=jax.ShapeDtypeStruct((planes, CELLS, bands), jnp.bfloat16),
-        in_specs=[vmem, vmem],
-        out_specs=vmem,
-        compiler_params=pltpu.CompilerParams(vmem_limit_bytes=32 * 2**20),
+        in_specs=[hbm, vmem],
+        out_specs=hbm,
+        scratch_shapes=[
+            pltpu.VMEM((planes, CELLS, bands), jnp.bfloat16),
+            pltpu.VMEM((planes, CELLS, bands), jnp.bfloat16),
+            pltpu.SemaphoreType.DMA,
+            pltpu.SemaphoreType.DMA((planes,)),
+        ],
+        compiler_params=pltpu.CompilerParams(vmem_limit_bytes=58 * 2**20),
         cost_estimate=pl.CostEstimate(
             flops=4 * 10**8, bytes_accessed=4 * 10**6, transcendentals=0
         ),

time: 108 us -> 102 us (0.944)
  local copies, waits for them, and re-layouts: 4 us -> 0 us
  Pallas kernels: 104 us -> 102 us
    unnamed x8 -> x0, local copies, waits for them, and re-layouts: 4 us -> none
    pallas_call x1, Pallas kernels: 84.3 us -> 80.8 us  [filtered_and_gram(): pl.pallas_call(functools.partial(filter_kernel, n, rows), out_shape=(jax....]
    pallas_call x1, Pallas kernels: 19.5 us -> 20.8 us  [shards(): pl.pallas_call(whiten_kernel, out_shape=jax.ShapeDtypeStruct((planes, CEL...]
where the time goes in v3:
time: 102 us
  Pallas kernels  102 us (100%)
    pallas_call x1, Pallas kernels, filtered_and_gram(): pl.pallas_call(functools.partial(filter_kernel, n, rows), out_shape=(jax....  80.8 us
    pallas_call x1, Pallas kernels, shards(): pl.pallas_call(whiten_kernel, out_shape=jax.ShapeDtypeStruct((planes, CEL...  20.8 us

profile of v3, /device:TPU:0, one launch (start us, length us, event | category | flops | bytes accessed | tf_op | source)
XLA Modules:
  0.0 101.8 jit_solution(5083076701184957537)
XLA Ops:
  0.0 80.8 %filter_gram.1 = (bf16[6,512,256]{2,1,0:T(8,128)(2,1)}, f32[3,128,128]{2,1,0:T(8,128)}) custom-call(s32[16]{0:T(128)} %dom.1, bf16[6,512,256]{2,1,0:T(8,128)(2,1)} %bitcast.2, f32[6,512]{1,0:T(8,128)} %pot.1, bf16[4,256,512]{2,1,0:T(8,128)(2,1)} %constant.2.clone.amat_hbm), custom_call_target="tpu_custom_call" | custom-call | flops 8000000000 | bytes 5000000 | tf_op jit(solution)/shard_map/filter_gram/pallas_call | solution.py:412
  80.9 20.8 %whiten.1 = bf16[6,512,256]{2,1,0:T(8,128)(2,1)} custom-call(bf16[6,512,256]{2,1,0:T(8,128)(2,1)} %get-tuple-element.7.fil_hbm, f32[3,128,128]{2,1,0:T(8,128)} %get-tuple-element.8.sums), custom_call_target="tpu_custom_call" | custom-call | flops 400000000 | bytes 4000000 | tf_op jit(solution)/shard_map/whiten/pallas_call | solution.py:532

commit v4 on v3

--- a/solution.py
+++ b/solution.py
@@ -42,11 +42,12 @@
 
 def filter_kernel(
     n, rows, dom, wav, pot, amat_hbm, fil_out, g_out,
-    wz, amat, ext, last, potb, diag, fil, acc, gsend, grecv, gback, gfin,
+    amat, ext0, ext1, ext2, ext3, last, potb, diag, fil, acc, gsend, grecv, gback, gfin,
     in_send, in_recv, pot_send, pot_recv, halo_send, halo_recv,
     out_send, out_recv, load, store, a_send, a_recv, b_send, b_recv,
 ):
     me = lax.axis_index("gz")
+    ext = (ext0, ext1, ext2, ext3)
     planes = wav.shape[0]
     own = 2 * planes
     quad = me // 4
@@ -76,12 +77,9 @@
         jnp.where(marks[1] == marks[2], 1.0, 0.0).astype(jnp.float32),
         jnp.where((marks[2] == marks[3]) & has_upper, 1.0, 0.0).astype(jnp.float32),
     ]
-    for plane in range(own):
-        for k in (1, 2, 3):
-            for place, other in enumerate((plane - k, plane + k)):
-                a, b = plane // planes, other // planes
-                weight = -0.5 * SCALE * COEF[k]
-                wz[plane, 2 * k - 2 + place] = ones[max(a, b)] * weight if a != b else weight
+    mid = ones[1]
+    far = jnp.where(core == 0, ones[0], ones[2])
+    near = jnp.where(core == 0, ones[2], ones[0])
 
     slot = r % 2
     starts = (HALO * slot, HALO * (1 - slot))
@@ -89,7 +87,7 @@
     def in_copy(h, piece, remote):
         start = starts[piece]
         src = wav.at[pl.ds(start, HALO), :, h * PANEL : (h + 1) * PANEL]
-        dst = ext.at[0, pl.ds(HALO + planes * slot + start, HALO)]
+        dst = ext0.at[pl.ds(HALO + planes * slot + start, HALO)]
         if remote:
             return pltpu.make_async_remote_copy(
                 src_ref=src, dst_ref=dst,
@@ -128,32 +126,32 @@
     @pl.when(jnp.logical_not(has_lower))
     def _():
         for step in range(DEGREE):
-            ext[step, 0:HALO] = jnp.zeros((HALO, CELLS, PANEL), jnp.bfloat16)
+            ext[step][0:HALO] = jnp.zeros((HALO, CELLS, PANEL), jnp.bfloat16)
 
     @pl.when(jnp.logical_not(has_upper))
     def _():
         for step in range(DEGREE):
-            ext[step, HALO + own : HALO + own + HALO] = jnp.zeros(
+            ext[step][HALO + own : HALO + own + HALO] = jnp.zeros(
                 (HALO, CELLS, PANEL), jnp.bfloat16
             )
 
     def in_wait(which, piece):
         start = HALO * which if piece == 0 else HALO * (1 - which)
-        dst = ext.at[0, pl.ds(HALO + planes * which + start, HALO)]
+        dst = ext0.at[pl.ds(HALO + planes * which + start, HALO)]
         pltpu.make_async_copy(dst, dst, in_recv.at[which, piece]).wait()
 
     def down_copy(step):
         return pltpu.make_async_remote_copy(
-            src_ref=ext.at[step, pl.ds(HALO, HALO)],
-            dst_ref=ext.at[step, pl.ds(HALO + own, HALO)],
+            src_ref=ext[step].at[pl.ds(HALO, HALO)],
+            dst_ref=ext[step].at[pl.ds(HALO + own, HALO)],
             send_sem=halo_send.at[step, 0], recv_sem=halo_recv.at[step, 0],
             device_id={"gz": lower_dev}, device_id_type=MESH,
         )
 
     def up_copy(step):
         return pltpu.make_async_remote_copy(
-            src_ref=ext.at[step, pl.ds(own, HALO)],
-            dst_ref=ext.at[step, pl.ds(0, HALO)],
+            src_ref=ext[step].at[pl.ds(own, HALO)],
+            dst_ref=ext[step].at[pl.ds(0, HALO)],
             send_sem=halo_send.at[step, 1], recv_sem=halo_recv.at[step, 1],
             device_id={"gz": upper_dev}, device_id_type=MESH,
         )
@@ -211,31 +209,58 @@
     in_wait(0, 1)
     in_wait(1, 1)
 
+    def inward(t):
+        return jnp.where(core == 0, t, own - 1 - t)
+
+    def z_terms(source, t, at):
+        total = None
+        for k in (1, 2, 3):
+            weight = -0.5 * SCALE * COEF[k]
+            outer, inner = (
+                source[HALO + inward(t + s), at, :].astype(jnp.float32) for s in (-k, k)
+            )
+            if t - k < 0:
+                term = outer * (far * weight) + inner * weight
+            elif t < planes <= t + k:
+                term = outer * weight + inner * (mid * weight)
+            elif t - k < planes <= t:
+                term = outer * (mid * weight) + inner * weight
+            elif t + k >= own:
+                term = outer * weight + inner * (near * weight)
+            else:
+                term = (outer + inner) * weight
+            total = term if total is None else total + term
+        return total
+
     def update(step, first, second):
-        pair = jnp.concatenate([ext[step, HALO + first], ext[step, HALO + second]], axis=1)
-        for tile in range(CELLS // TILE):
+        source = ext[step]
+        pair = jnp.concatenate(
+            [source[HALO + inward(first)], source[HALO + inward(second)]], axis=1
+        )
+
+        def products(tile):
+            return jnp.dot(amat[tile], pair, preferred_element_type=jnp.float32)
+
+        tiles = CELLS // TILE
+        ready = products(0)
+        for tile in range(tiles):
             at = slice(tile * TILE, (tile + 1) * TILE)
-            both = jnp.dot(amat[tile], pair, preferred_element_type=jnp.float32)
+            both = ready
+            if tile + 1 < tiles:
+                ready = products(tile + 1)
             image = both[:TILE] + both[TILE:]
-            for place, plane in enumerate((first, second)):
+            for place, t in enumerate((first, second)):
+                plane = inward(t)
                 value = image[:, place * PANEL : (place + 1) * PANEL]
-                centre = ext[step, HALO + plane, at, :].astype(jnp.float32)
-                value = value + diag[plane, at, :] * centre
-                for k in (1, 2, 3):
-                    value = value + wz[plane, 2 * k - 2] * ext[
-                        step, HALO + plane - k, at, :
-                    ].astype(jnp.float32)
-                    value = value + wz[plane, 2 * k - 1] * ext[
-                        step, HALO + plane + k, at, :
-                    ].astype(jnp.float32)
+                centre = source[HALO + plane, at, :].astype(jnp.float32)
+                value = value + diag[plane, at, :] * centre + z_terms(source, t, at)
                 if step == 0:
                     value = value * 0.5
                 else:
-                    older = ext[step - 1, HALO + plane, at, :].astype(jnp.float32)
-                    value = value - older
+                    value = value - ext[step - 1][HALO + plane, at, :].astype(jnp.float32)
                 value = value.astype(jnp.bfloat16)
                 if step < DEGREE - 1:
-                    ext[step + 1, HALO + plane, at, :] = value
+                    ext[step + 1][HALO + plane, at, :] = value
                 else:
                     last[plane, at, :] = value
 
@@ -263,13 +288,9 @@
         def _():
             out_copy(part, False).start()
 
-    def inward(t):
-        return jnp.where(core == 0, t, own - 1 - t)
-
     def update_pairs(step, start, count):
-        @pl.loop(0, count)
-        def _(j):
-            update(step, inward(start + 2 * j), inward(start + 2 * j + 1))
+        for j in range(count):
+            update(step, start + 2 * j, start + 2 * j + 1)
 
     for step in range(DEGREE):
         final = step == DEGREE - 1
@@ -408,6 +429,7 @@
     smem = pl.BlockSpec(memory_space=pltpu.SMEM)
     hbm = pl.BlockSpec(memory_space=pl.ANY)
     dma = pltpu.SemaphoreType.DMA
+    wide = pltpu.VMEM((own + 2 * HALO, CELLS, PANEL), jnp.bfloat16)
     chunk = pltpu.VMEM((n, 3, rows, PANEL), jnp.float32)
     return pl.pallas_call(
         functools.partial(filter_kernel, n, rows),
@@ -418,9 +440,8 @@
         in_specs=[smem, hbm, hbm, hbm],
         out_specs=(hbm, vmem),
         scratch_shapes=[
-            pltpu.SMEM((own, 6), jnp.float32),
             pltpu.VMEM((CELLS // TILE, 2 * TILE, CELLS), jnp.bfloat16),
-            pltpu.VMEM((DEGREE, own + 2 * HALO, CELLS, PANEL), jnp.bfloat16),
+            wide, wide, wide, wide,
             pltpu.VMEM((own, CELLS, PANEL), jnp.bfloat16),
             pltpu.VMEM((2, planes, CELLS), jnp.float32),
             pltpu.VMEM((own, CELLS, PANEL), jnp.float32),
@@ -471,12 +492,13 @@
             scale = jnp.where(row == j, over, scale)
             if j == BLOCK - 1:
                 break
-            factor = jnp.where(row > j, pivot_columns[j] * over, 0.0)
+            column = jnp.where(row > j, pivot_columns[j], 0.0)
             for later in range(j + 1, BLOCK):
-                pivot_columns[later] = pivot_columns[later] - factor * jnp.broadcast_to(
+                product = column * jnp.broadcast_to(
                     pivot_columns[later][j : j + 1], (BLOCK, PANEL)
                 )
-            top = top - factor * jnp.broadcast_to(top[j : j + 1], (BLOCK, PANEL))
+                pivot_columns[later] = pivot_columns[later] - product * over
+            top = top - (column * jnp.broadcast_to(top[j : j + 1], (BLOCK, PANEL))) * over
         end = start + BLOCK
         result.append(jnp.where(lane < end, top * jnp.sqrt(scale), 0.0))
         if end < PANEL:

time: 102 us -> 98.1 us (0.962)
  Pallas kernels: 102 us -> 97.8 us
    pallas_call x1, Pallas kernels: 80.8 us -> 77.7 us  [filtered_and_gram(): pl.pallas_call(functools.partial(filter_kernel, n, rows), out_shape=(jax....]
where the time goes in v4:
time: 98.1 us; the launch traced here: 97.9 us
  Pallas kernels  97.8 us (100%)
    pallas_call x1, Pallas kernels, filtered_and_gram(): pl.pallas_call(functools.partial(filter_kernel, n, rows), out_shape=(jax....  77.7 us
    pallas_call x1, Pallas kernels, shards(): pl.pallas_call(whiten_kernel, out_shape=jax.ShapeDtypeStruct((planes, CEL...  20.1 us

profile of v4, /device:TPU:0, one launch (start us, length us, event | category | flops | bytes accessed | tf_op | source)
XLA Modules:
  0.0 97.9 jit_solution(16947517327174991401)
XLA Ops:
  0.0 77.7 %filter_gram.1 = (bf16[6,512,256]{2,1,0:T(8,128)(2,1)}, f32[3,128,128]{2,1,0:T(8,128)}) custom-call(s32[16]{0:T(128)} %dom.1, bf16[6,512,256]{2,1,0:T(8,128)(2,1)} %bitcast.2, f32[6,512]{1,0:T(8,128)} %pot.1, bf16[4,256,512]{2,1,0:T(8,128)(2,1)} %constant.2.clone.amat_hbm), custom_call_target="tpu_custom_call" | custom-call | flops 8000000000 | bytes 5000000 | tf_op jit(solution)/shard_map/filter_gram/pallas_call | solution.py:434
  77.7 20.1 %whiten.1 = bf16[6,512,256]{2,1,0:T(8,128)(2,1)} custom-call(bf16[6,512,256]{2,1,0:T(8,128)(2,1)} %get-tuple-element.7.fil_hbm, f32[3,128,128]{2,1,0:T(8,128)} %get-tuple-element.8.sums), custom_call_target="tpu_custom_call" | custom-call | flops 400000000 | bytes 4000000 | tf_op jit(solution)/shard_map/whiten/pallas_call | solution.py:554

commit v5 on v4

--- a/solution.py
+++ b/solution.py
@@ -68,6 +68,21 @@
             barrier, inc=1, device_id={"gz": (me + off) % n}, device_id_type=MESH
         )
 
+    amat_copy = pltpu.make_async_copy(amat_hbm, amat, load)
+    amat_copy.start()
+
+    @pl.when(jnp.logical_not(has_lower))
+    def _():
+        for step in range(DEGREE):
+            ext[step][0:HALO] = jnp.zeros((HALO, CELLS, PANEL), jnp.bfloat16)
+
+    @pl.when(jnp.logical_not(has_upper))
+    def _():
+        for step in range(DEGREE):
+            ext[step][HALO + own : HALO + own + HALO] = jnp.zeros(
+                (HALO, CELLS, PANEL), jnp.bfloat16
+            )
+
     pl.semaphore_wait(barrier, n - 1)
 
     first = quad * 4 + core * 2
@@ -105,7 +120,6 @@
             )
         return pltpu.make_async_copy(pot, potb.at[slot], pot_recv.at[slot])
 
-    amat_copy = pltpu.make_async_copy(amat_hbm, amat, load)
     for h in (0, 1):
         away = quad * 4 + 2 * h + half != me
 
@@ -120,20 +134,6 @@
             in_copy(h, 0, False).start()
             pot_copy(h, False).start()
             in_copy(h, 1, False).start()
-
-    amat_copy.start()
-
-    @pl.when(jnp.logical_not(has_lower))
-    def _():
-        for step in range(DEGREE):
-            ext[step][0:HALO] = jnp.zeros((HALO, CELLS, PANEL), jnp.bfloat16)
-
-    @pl.when(jnp.logical_not(has_upper))
-    def _():
-        for step in range(DEGREE):
-            ext[step][HALO + own : HALO + own + HALO] = jnp.zeros(
-                (HALO, CELLS, PANEL), jnp.bfloat16
-            )
 
     def in_wait(which, piece):
         start = HALO * which if piece == 0 else HALO * (1 - which)
@@ -339,12 +339,7 @@
             acc[1] += gram[0:PANEL, PANEL:]
             acc[2] += gram[PANEL:, PANEL:]
 
-    @pl.loop(0, n)
-    def _(j):
-        at = pl.ds(pl.multiple_of(j * rows, rows), rows)
-        gsend[j] = acc[:, at, :]
-
-    def exchange(src, dst, send, recv):
+    def exchange(make, src, dst, send, recv):
         def copy(target, origin):
             return pltpu.make_async_remote_copy(
                 src_ref=src.at[target], dst_ref=dst.at[origin],
@@ -354,18 +349,20 @@
 
         @pl.loop(1, n)
         def _(off):
-            copy((me + off) % n, me).start()
-
-        dst[me] = src[me]
+            there = (me + off) % n
+            src[there] = make(there)
+            copy(there, me).start()
+
+        dst[me] = make(me)
 
         @pl.loop(1, n)
         def _(off):
             copy((me + off) % n, (me + off) % n).wait_recv()
 
-    exchange(gsend, grecv, a_send, a_recv)
-
-    @pl.loop(0, n)
-    def _(j):
+    def row_chunk(j):
+        return acc[:, pl.ds(pl.multiple_of(j * rows, rows), rows), :]
+
+    def domain_mean(j):
         mark = dom[j]
 
         def add(i, sums):
@@ -374,11 +371,13 @@
             return total + same * grecv[i], blocks + same
 
         zero = jnp.zeros((3, rows, PANEL), jnp.float32)
-        total, blocks = lax.fori_loop(0, n, add, (zero, jnp.float32(0.0)), unroll=8)
-        size = jnp.full((3, rows, PANEL), blocks * (planes * CELLS), jnp.float32)
-        gback[j] = total / size
-
-    exchange(gback, gfin, b_send, b_recv)
+        total, blocks = lax.fori_loop(
+            0, n, add, (zero, jnp.float32(0.0)), unroll=min(n, 16)
+        )
+        return total / jnp.full((3, rows, PANEL), blocks * (planes * CELLS), jnp.float32)
+
+    exchange(row_chunk, gsend, grecv, a_send, a_recv)
+    exchange(domain_mean, gback, gfin, b_send, b_recv)
 
     @pl.loop(0, n)
     def _(j):
@@ -462,7 +461,7 @@
     )(domain_of, waves, potential, jnp.asarray(plane_matrix()))
 
 
-BLOCK = 8
+BLOCK = 16
 
 
 def exact(a, b, contract=((1,), (0,))):
@@ -472,12 +471,14 @@
     )
 
 
-def inverse_factor(gram):
+def inverse_factor(gram, beside=None):
     row = lax.broadcasted_iota(jnp.int32, (BLOCK, PANEL), 0)
     lane = lax.broadcasted_iota(jnp.int32, (BLOCK, PANEL), 1)
     rest = gram
     result = []
     for start in range(0, PANEL, BLOCK):
+        if beside is not None:
+            beside(start // BLOCK, PANEL // BLOCK)
         top = rest[:BLOCK]
         inside = (lane >= start) & (lane < start + BLOCK)
         pivot_columns = [
@@ -510,7 +511,7 @@
     return jnp.concatenate(result, axis=0)
 
 
-def whiten_kernel(fil_hbm, sums, out_hbm, fil, out, load, store):
+def whiten_kernel(fil_hbm, sums, out_hbm, fil, out, reduced, load, store):
     load_copy = pltpu.make_async_copy(fil_hbm, fil, load)
     load_copy.start()
     g00, g01, g11 = sums[0], sums[1], sums[2]
@@ -521,20 +522,29 @@
     cf = corr_r.astype(jnp.float32)
     middle = exact(exact(exact(w0f, g00), w0f, ((1,), (1,))), cf) - corr
     gram1 = g11 + exact(cf, middle, ((0,), (0,))) - exact(corr, cf, ((0,), (0,)))
-    w1 = inverse_factor(gram1).astype(jnp.bfloat16)
+    load_copy.wait()
+    planes = fil.shape[0]
 
     def times(a, b, contract):
         return lax.dot_general(a, b, (contract, ((), ())), preferred_element_type=jnp.float32)
 
-    load_copy.wait()
-
-    @pl.loop(0, fil.shape[0])
+    chunks = [(i, t * TILE) for i in range(planes) for t in range(CELLS // TILE)]
+
+    def reduce_some(place, blocks):
+        share = -(-len(chunks) // blocks)
+        for i, start in chunks[place * share : (place + 1) * share]:
+            at = slice(start, start + TILE)
+            e0 = times(fil[i, at, :PANEL], w0, ((1,), (1,))).astype(jnp.bfloat16)
+            out[i, at, :PANEL] = e0
+            b1 = fil[i, at, PANEL:].astype(jnp.float32)
+            left = (b1 - times(e0, corr_r, ((1,), (0,)))).astype(jnp.bfloat16)
+            reduced[i, at, :] = left
+
+    w1 = inverse_factor(gram1, reduce_some).astype(jnp.bfloat16)
+
+    @pl.loop(0, planes)
     def _(i):
-        e0 = times(fil[i, :, :PANEL], w0, ((1,), (1,))).astype(jnp.bfloat16)
-        out[i, :, :PANEL] = e0
-        b1 = fil[i, :, PANEL:].astype(jnp.float32)
-        reduced = (b1 - times(e0, corr_r, ((1,), (0,)))).astype(jnp.bfloat16)
-        out[i, :, PANEL:] = times(reduced, w1, ((1,), (1,))).astype(jnp.bfloat16)
+        out[i, :, PANEL:] = times(reduced[i], w1, ((1,), (1,))).astype(jnp.bfloat16)
         pltpu.make_async_copy(out.at[i], out_hbm.at[i], store.at[i]).start()
 
     @pl.loop(0, fil.shape[0])
@@ -559,6 +569,7 @@
         scratch_shapes=[
             pltpu.VMEM((planes, CELLS, bands), jnp.bfloat16),
             pltpu.VMEM((planes, CELLS, bands), jnp.bfloat16),
+            pltpu.VMEM((planes, CELLS, PANEL), jnp.bfloat16),
             pltpu.SemaphoreType.DMA,
             pltpu.SemaphoreType.DMA((planes,)),
         ],

time: 98.1 us -> 90.4 us (0.922)
  Pallas kernels: 97.8 us -> 89.9 us
    pallas_call x1, Pallas kernels: 20.1 us -> 13 us  [shards(): pl.pallas_call(whiten_kernel, out_shape=jax.ShapeDtypeStruct((planes, CEL...]
where the time goes in v5:
time: 90.4 us; the launch traced here: 90.1 us
  Pallas kernels  89.9 us (99%)
    pallas_call x1, Pallas kernels, filtered_and_gram(): pl.pallas_call(functools.partial(filter_kernel, n, rows), out_shape=(jax....  76.9 us
    pallas_call x1, Pallas kernels, shards(): pl.pallas_call(whiten_kernel, out_shape=jax.ShapeDtypeStruct((planes, CEL...  13 us

profile of v5, /device:TPU:0, one launch (start us, length us, event | category | flops | bytes accessed | tf_op | source)
XLA Modules:
  0.0 90.1 jit_solution(12932404565068383051)
XLA Ops:
  0.0 76.9 %filter_gram.1 = (bf16[6,512,256]{2,1,0:T(8,128)(2,1)}, f32[3,128,128]{2,1,0:T(8,128)}) custom-call(s32[16]{0:T(128)} %dom.1, bf16[6,512,256]{2,1,0:T(8,128)(2,1)} %bitcast.2, f32[6,512]{1,0:T(8,128)} %pot.1, bf16[4,256,512]{2,1,0:T(8,128)(2,1)} %constant.2.clone.amat_hbm), custom_call_target="tpu_custom_call" | custom-call | flops 8000000000 | bytes 5000000 | tf_op jit(solution)/shard_map/filter_gram/pallas_call | solution.py:433
  76.9 13.0 %whiten.1 = bf16[6,512,256]{2,1,0:T(8,128)(2,1)} custom-call(bf16[6,512,256]{2,1,0:T(8,128)(2,1)} %get-tuple-element.7.fil_hbm, f32[3,128,128]{2,1,0:T(8,128)} %get-tuple-element.8.sums), custom_call_target="tpu_custom_call" | custom-call | flops 400000000 | bytes 4000000 | tf_op jit(solution)/shard_map/whiten/pallas_call | solution.py:564

commit v6 on v5

--- a/solution.py
+++ b/solution.py
@@ -140,57 +140,67 @@
         dst = ext0.at[pl.ds(HALO + planes * which + start, HALO)]
         pltpu.make_async_copy(dst, dst, in_recv.at[which, piece]).wait()
 
-    def down_copy(step):
+    def down_copy(step, piece):
+        start, count = ((0, 2), (2, 1))[piece]
         return pltpu.make_async_remote_copy(
-            src_ref=ext[step].at[pl.ds(HALO, HALO)],
-            dst_ref=ext[step].at[pl.ds(HALO + own, HALO)],
-            send_sem=halo_send.at[step, 0], recv_sem=halo_recv.at[step, 0],
+            src_ref=ext[step].at[pl.ds(HALO + start, count)],
+            dst_ref=ext[step].at[pl.ds(HALO + own + start, count)],
+            send_sem=halo_send.at[step, 0, piece], recv_sem=halo_recv.at[step, 0, piece],
             device_id={"gz": lower_dev}, device_id_type=MESH,
         )
 
-    def up_copy(step):
+    def up_copy(step, piece):
+        start, count = ((1, 2), (0, 1))[piece]
         return pltpu.make_async_remote_copy(
-            src_ref=ext[step].at[pl.ds(own, HALO)],
-            dst_ref=ext[step].at[pl.ds(0, HALO)],
-            send_sem=halo_send.at[step, 1], recv_sem=halo_recv.at[step, 1],
+            src_ref=ext[step].at[pl.ds(own + start, count)],
+            dst_ref=ext[step].at[pl.ds(start, count)],
+            send_sem=halo_send.at[step, 1, piece], recv_sem=halo_recv.at[step, 1, piece],
             device_id={"gz": upper_dev}, device_id_type=MESH,
         )
 
-    def send_far(step):
+    def send_far(step, pieces=(0, 1)):
         @pl.when((core == 0) & has_lower)
         def _():
-            down_copy(step).start()
+            for piece in pieces:
+                down_copy(step, piece).start()
 
         @pl.when((core == 1) & has_upper)
         def _():
-            up_copy(step).start()
+            for piece in pieces:
+                up_copy(step, piece).start()
 
     def send_near(step):
         @pl.when(core == 0)
         def _():
-            up_copy(step).start()
+            for piece in (0, 1):
+                up_copy(step, piece).start()
 
         @pl.when(core == 1)
         def _():
-            down_copy(step).start()
+            for piece in (0, 1):
+                down_copy(step, piece).start()
 
     def wait_far(step):
         @pl.when((core == 0) & has_lower)
         def _():
-            up_copy(step).wait_recv()
+            for piece in (0, 1):
+                up_copy(step, piece).wait_recv()
 
         @pl.when((core == 1) & has_upper)
         def _():
-            down_copy(step).wait_recv()
+            for piece in (0, 1):
+                down_copy(step, piece).wait_recv()
 
     def wait_near(step):
         @pl.when(core == 0)
         def _():
-            down_copy(step).wait_recv()
+            for piece in (0, 1):
+                down_copy(step, piece).wait_recv()
 
         @pl.when(core == 1)
         def _():
-            up_copy(step).wait_recv()
+            for piece in (0, 1):
+                up_copy(step, piece).wait_recv()
 
     in_wait(core, 0)
     send_far(0)
@@ -304,12 +314,15 @@
         if final:
             send_out(2)
         wait_far(step)
-        update_pairs(step, 0, 2)
+        update_pairs(step, 0, 1)
+        if not final:
+            send_far(step + 1, (0,))
+        update_pairs(step, 2, 1)
         if final:
             send_out(0)
             send_out(1)
         else:
-            send_far(step + 1)
+            send_far(step + 1, (1,))
 
     def out_wait(h, piece):
         dst = fil.at[h, pl.ds(HALO * piece, HALO)]
@@ -406,11 +419,13 @@
 
         @pl.when(has_lower)
         def _(step=step):
-            down_copy(step).wait_send()
+            for piece in (0, 1):
+                down_copy(step, piece).wait_send()
 
         @pl.when(has_upper)
         def _(step=step):
-            up_copy(step).wait_send()
+            for piece in (0, 1):
+                up_copy(step, piece).wait_send()
 
     @pl.loop(1, n)
     def _(off):
@@ -448,7 +463,7 @@
             pltpu.VMEM((3, PANEL, PANEL), jnp.float32),
             chunk, chunk, chunk, chunk,
             dma((2, 2)), dma((2, 2)), dma((2,)), dma((2,)),
-            dma((DEGREE, 2)), dma((DEGREE, 2)), dma((4,)), dma((2, 2)), dma, dma((2, 2)),
+            dma((DEGREE, 2, 2)), dma((DEGREE, 2, 2)), dma((4,)), dma((2, 2)), dma, dma((2, 2)),
             dma((n,)), dma((n,)), dma((n,)), dma((n,)),
         ],
         compiler_params=pltpu.CompilerParams(

time: 90.4 us -> 90.1 us (level)
  no operation moved by 1% of the time
where the time goes in v6:
time: 90.1 us; the launch traced here: 89.8 us
  Pallas kernels  89.6 us (99%)
    pallas_call x1, Pallas kernels, filtered_and_gram(): pl.pallas_call(functools.partial(filter_kernel, n, rows), out_shape=(jax....  76.5 us
    pallas_call x1, Pallas kernels, shards(): pl.pallas_call(whiten_kernel, out_shape=jax.ShapeDtypeStruct((planes, CEL...  13 us

profile of v6, /device:TPU:0, one launch (start us, length us, event | category | flops | bytes accessed | tf_op | source)
XLA Modules:
  0.0 89.8 jit_solution(114449009259388503)
XLA Ops:
  0.0 76.5 %filter_gram.1 = (bf16[6,512,256]{2,1,0:T(8,128)(2,1)}, f32[3,128,128]{2,1,0:T(8,128)}) custom-call(s32[16]{0:T(128)} %dom.1, bf16[6,512,256]{2,1,0:T(8,128)(2,1)} %bitcast.2, f32[6,512]{1,0:T(8,128)} %pot.1, bf16[4,256,512]{2,1,0:T(8,128)(2,1)} %constant.2.clone.amat_hbm), custom_call_target="tpu_custom_call" | custom-call | flops 8000000000 | bytes 5000000 | tf_op jit(solution)/shard_map/filter_gram/pallas_call | solution.py:448
  76.5 13.0 %whiten.1 = bf16[6,512,256]{2,1,0:T(8,128)(2,1)} custom-call(bf16[6,512,256]{2,1,0:T(8,128)(2,1)} %get-tuple-element.7.fil_hbm, f32[3,128,128]{2,1,0:T(8,128)} %get-tuple-element.8.sums), custom_call_target="tpu_custom_call" | custom-call | flops 400000000 | bytes 4000000 | tf_op jit(solution)/shard_map/whiten/pallas_call | solution.py:579
